TPU v7x, 32 devices: a whole 2x2x4 slice. The times are simulated.
32 devices in a mesh: patch: 8 (over z, y), rep: 4 (over x, core).
Axes of the slice: x: 2, y: 2, z: 4, core: 2. Of those that a mesh axis runs over, the one named last changes fastest.
Arguments:
- previous_state: float32 [4, 84, 24576], P('rep', None, 'patch'), may hold values from -6 to 6
- target_state: float32 [4, 84, 24576], P('rep', None, 'patch'), may hold values from -6 to 6
- noise_draws: float32 [4, 2, 84, 24576], P('rep', None, None, 'patch'), may hold values from -6 to 6
- noise_level: float32 [4, 2], P('rep'), may hold values from 0.3 to 3
- pixel_owner: int32 [4, 24576], P('rep', 'patch'), may hold values from 0 to 511, as said below
- mesh_to_grid: int32 [4, 3, 24576], P('rep', None, 'patch'), may hold values from 0 to 511, as said below
- neighbours: int32 [4, 4096, 16], P('rep', 'patch'), may hold values from 0 to 639, as said below
- halo_send: int32 [4, 1024], P('rep', 'patch'), may hold values from 0 to 511, as said below
- node_count: int32 [4, 8], P('rep', 'patch'), may hold values from 106 to 512, as said below
- pixel_count: int32 [4, 8], P('rep', 'patch'), may hold values from 640 to 3072, as said below
- w_encode: float32 [168, 512], P(None, ('patch', 'rep')), may hold values from -0.5 to 0.5
- w_project: float32 [512, 1536], P(('patch', 'rep')), may hold values from -0.25 to 0.25
- w_output: float32 [512, 512], P(('patch', 'rep')), may hold values from -0.5 to 0.5
- w_up: float32 [512, 2048], P(('patch', 'rep')), may hold values from -0.25 to 0.25
- w_down: float32 [2048, 512], P(('patch', 'rep')), may hold values from -0.125 to 0.125
- w_noise: float32 [32, 2048], P(None, ('patch', 'rep')), may hold values from -1 to 1
- w_decode: float32 [512, 84], P(('patch', 'rep')), may hold values from -0.25 to 0.25
- m_encode: float32 [168, 512], P(None, ('patch', 'rep')), may hold values from -0.00036621094 to 0.00036621094
- m_project: float32 [512, 1536], P(('patch', 'rep')), may hold values from -0.00036621094 to 0.00036621094
- m_output: float32 [512, 512], P(('patch', 'rep')), may hold values from -0.00036621094 to 0.00036621094
- m_up: float32 [512, 2048], P(('patch', 'rep')), may hold values from -0.00036621094 to 0.00036621094
- m_down: float32 [2048, 512], P(('patch', 'rep')), may hold values from -0.00036621094 to 0.00036621094
- m_noise: float32 [32, 2048], P(None, ('patch', 'rep')), may hold values from -0.00036621094 to 0.00036621094
- m_decode: float32 [512, 84], P(('patch', 'rep')), may hold values from -0.00036621094 to 0.00036621094
- v_encode: float32 [168, 512], P(None, ('patch', 'rep')), may hold values from 1.5747146e-08 to 6.286883e-08
- v_project: float32 [512, 1536], P(('patch', 'rep')), may hold values from 1.5747146e-08 to 6.286883e-08
- v_output: float32 [512, 512], P(('patch', 'rep')), may hold values from 1.5747146e-08 to 6.286883e-08
- v_up: float32 [512, 2048], P(('patch', 'rep')), may hold values from 1.5747146e-08 to 6.286883e-08
- v_down: float32 [2048, 512], P(('patch', 'rep')), may hold values from 1.5747146e-08 to 6.286883e-08
- v_noise: float32 [32, 2048], P(None, ('patch', 'rep')), may hold values from 1.5747146e-08 to 6.286883e-08
- v_decode: float32 [512, 84], P(('patch', 'rep')), may hold values from 1.5747146e-08 to 6.286883e-08
Outputs:
- new_encode: float32 [168, 512], P(None, ('patch', 'rep'))
- new_project: float32 [512, 1536], P(('patch', 'rep'))
- new_output: float32 [512, 512], P(('patch', 'rep'))
- new_up: float32 [512, 2048], P(('patch', 'rep'))
- new_down: float32 [2048, 512], P(('patch', 'rep'))
- new_noise: float32 [32, 2048], P(None, ('patch', 'rep'))
- new_decode: float32 [512, 84], P(('patch', 'rep'))
- moment_encode: float32 [168, 512], P(None, ('patch', 'rep'))
- moment_project: float32 [512, 1536], P(('patch', 'rep'))
- moment_output: float32 [512, 512], P(('patch', 'rep'))
- moment_up: float32 [512, 2048], P(('patch', 'rep'))
- moment_down: float32 [2048, 512], P(('patch', 'rep'))
- moment_noise: float32 [32, 2048], P(None, ('patch', 'rep'))
- moment_decode: float32 [512, 84], P(('patch', 'rep'))
- second_encode: float32 [168, 512], P(None, ('patch', 'rep'))
- second_project: float32 [512, 1536], P(('patch', 'rep'))
- second_output: float32 [512, 512], P(('patch', 'rep'))
- second_up: float32 [512, 2048], P(('patch', 'rep'))
- second_down: float32 [2048, 512], P(('patch', 'rep'))
- second_noise: float32 [32, 2048], P(None, ('patch', 'rep'))
- second_decode: float32 [512, 84], P(('patch', 'rep'))
- loss_sum: float32 [], replicated
- count_total: float32 [], replicated
- grad_norm: float32 [], replicated
Inputs may be any that keep to these rules, and one draw needn't show every extreme that they name: `pixel_owner`: names only live nodes of the pixel's patch. `mesh_to_grid`: names only live nodes of the pixel's patch. `neighbours`: entry 0 of each node's list is the node itself; entries of 512 or more name halo rows (lower patch's first). `halo_send`: only live nodes of the sending patch are named. `node_count`: the last patch of every sample is full. `pixel_count`: the last patch of every sample is full.
All inputs are finite; a program needn't handle non-finite values.
Results may differ from a plain program's by a relative error of at most 0.011.
Values may be sent and summed in bfloat16 or wider, within the bound.
A program may use at most 256 MiB of HBM per device.

v0:
```python
import functools
import types

import jax
import jax.numpy as jnp
from jax import lax
from jax.experimental import pallas as pl
from jax.experimental.pallas import tpu as pltpu
from jax.sharding import PartitionSpec as P

HEADS = 4
HD = 128
FOUR = 32
NEIGH = 16
STEP = 5


LEARN_RATE = 0.03
BETA_ONE = 0.9
BETA_TWO = 0.95
EPSILON = 1e-08
DECAY_RATE = 0.1
THRESHOLD = 1.0

BOTH = ("patch", "rep")
LOW = jnp.bfloat16
WIDE = jnp.float32
SCALE = HD ** (-0.5)
VMEM_LIMIT = 62 * 2**20


def nn(a, b):
    return lax.dot_general(a, b, (((1,), (0,)), ((), ())), preferred_element_type=WIDE)


def nt(a, b):
    return lax.dot_general(a, b, (((1,), (1,)), ((), ())), preferred_element_type=WIDE)


def tn(a, b):
    return lax.dot_general(a, b, (((0,), (0,)), ((), ())), preferred_element_type=WIDE)


def fourier(level):
    frequency = 0.25 * (jnp.arange(FOUR // 2).astype(jnp.float32) + 1.0)
    angles = jnp.log(level) * frequency
    return jnp.concatenate([jnp.sin(angles), jnp.cos(angles)])


def norm_parts(hidden):
    centre = hidden - jnp.mean(hidden, axis=-1, keepdims=True)
    spread = jnp.mean(centre * centre, axis=-1, keepdims=True)
    inverse = lax.rsqrt(spread + 1e-05)
    return centre * inverse, inverse


MESH = pl.DeviceIdType.MESH
GRID = (4, 2, 2, 2)


def places():
    patch, rep = lax.axis_index("patch"), lax.axis_index("rep")
    z, y, x, c = patch // 2, patch % 2, rep // 2, rep % 2
    sibling = {"patch": patch, "rep": x * 2 + (1 - c)}
    across_x = {"patch": patch, "rep": (1 - x) * 2 + c}
    across_y = {"patch": z * 2 + (1 - y), "rep": rep}
    along_z = [{"patch": ((z + d) % 4) * 2 + y, "rep": rep} for d in range(4)]
    return z, y, x, c, sibling, across_x, across_y, along_z


def greet(others):
    barrier = pltpu.get_barrier_semaphore()
    for other in others:
        pl.semaphore_signal(barrier, inc=1, device_id=other, device_id_type=MESH)
    pl.semaphore_wait(barrier, len(others))


def send(src, dst, sems, index, device):
    copy = pltpu.make_async_remote_copy(
        src_ref=src, dst_ref=dst, send_sem=sems.at[(0,) + index], recv_sem=sems.at[(1,) + index],
        device_id=device, device_id_type=MESH,
    )
    copy.start()
    return copy


def plus(*terms):
    total = terms[0].astype(WIDE)
    for term in terms[1:]:
        total = total + term.astype(WIDE)
    return total


def scatter_scratch(rows, cols):
    h = cols // 2
    return [
        pltpu.VMEM((4, 2, 2, rows, cols), LOW),
        pltpu.VMEM((4, 2, 2, rows, cols), LOW),
        pltpu.VMEM((4, 2, rows, h), LOW),
        pltpu.VMEM((4, 2, rows, h), LOW),
        pltpu.VMEM((4, rows, h), LOW),
        pltpu.VMEM((4, 2, rows, h), LOW),
        pltpu.VMEM((4, 2, rows, h), LOW),
        pltpu.VMEM((4, rows, h), LOW),
        pltpu.VMEM((3, rows, cols), LOW),
        pltpu.VMEM((3, rows, cols), LOW),
    ]


def scatter_kernel(g_one, g_two, extra, out_one, out_two, totals, *scratch):
    z, y, x, c, sibling, across_x, across_y, along_z = places()
    parts = ((g_one, out_one) + scratch[:10], (g_two, out_two) + scratch[10:20])
    board, sems, small = scratch[20:]
    greet([sibling, across_x, across_y] + along_z[1:])
    steps = [(d, (z + d) % 4) for d in (1, 2, 3, 0)]
    sent, first, left, right, left_two, right_two, last = [], {}, {}, {}, {}, {}, {}
    for d, zd in steps:
        for i, (g, out, near, acc, near_l, acc_l, end_l, near_r, acc_r, end_r, going, come) in enumerate(parts):
            first[d, i] = send(g.at[zd, :, :, 1 - c], near.at[zd], sems, (0, d, i), sibling)
    for d, zd in steps:
        for i, (g, out, near, acc, near_l, acc_l, end_l, near_r, acc_r, end_r, going, come) in enumerate(parts):
            h = g.shape[-1] // 2
            first[d, i].wait_recv()
            acc[zd] = plus(g[zd, :, :, c], near[zd]).astype(LOW)
            left[d, i] = send(acc.at[zd, :, 1 - x, :, :h], near_l.at[zd], sems, (1, d, i), across_x)
            right[d, i] = send(acc.at[zd, 1 - y, :, :, h:], near_r.at[zd], sems, (2, d, i), across_y)
    for d, zd in steps:
        for i, (g, out, near, acc, near_l, acc_l, end_l, near_r, acc_r, end_r, going, come) in enumerate(parts):
            h = g.shape[-1] // 2
            left[d, i].wait_recv()
            acc_l[zd] = plus(acc[zd, :, x, :, :h], near_l[zd]).astype(LOW)
            left_two[d, i] = send(acc_l.at[zd, 1 - y], end_l.at[zd], sems, (3, d, i), across_y)
            right[d, i].wait_recv()
            acc_r[zd] = plus(acc[zd, y, :, :, h:], near_r[zd]).astype(LOW)
            right_two[d, i] = send(acc_r.at[zd, 1 - x], end_r.at[zd], sems, (4, d, i), across_x)
    for d, zd in steps:
        for i, (g, out, near, acc, near_l, acc_l, end_l, near_r, acc_r, end_r, going, come) in enumerate(parts):
            h = g.shape[-1] // 2
            left_two[d, i].wait_recv()
            done_l = plus(acc_l[zd, y], end_l[zd])
            right_two[d, i].wait_recv()
            done_r = plus(acc_r[zd, x], end_r[zd])
            if d == 0:
                out[:, :h] = done_l
                out[:, h:] = done_r
            else:
                going[d - 1, :, :h] = done_l.astype(LOW)
                going[d - 1, :, h:] = done_r.astype(LOW)
                last[d, i] = send(going.at[d - 1], come.at[d - 1], sems, (5, d, i), along_z[d])
    squares = jnp.zeros((), WIDE)
    for i, part in enumerate(parts):
        out, come = part[1], part[11]
        for d in (1, 2, 3):
            last[d, i].wait_recv()
        out[...] = plus(out[...], come[0], come[1], come[2])
        squares = squares + jnp.sum(out[...] * out[...])
    row = lax.broadcasted_iota(jnp.int32, extra.shape, 0)
    board[0] = jnp.where(row == 0, squares, extra[...])
    more = []
    for phase, device in enumerate((sibling, across_x, across_y)):
        copy = send(board.at[phase], board.at[4 + phase], small, (phase,), device)
        copy.wait_recv()
        more.append(copy)
        board[phase + 1] = board[phase] + board[4 + phase]
    for d in (1, 2, 3):
        more.append(send(board.at[3], board.at[8 + z], small, (2 + d,), along_z[d]))
    board[8 + z] = board[3]
    for d in (1, 2, 3):
        more[2 + d].wait_recv()
    totals[...] = board[8] + board[9] + board[10] + board[11]
    for group in (first, left, right, left_two, right_two, last):
        for copy in group.values():
            copy.wait_send()
    for copy in more:
        copy.wait_send()


def reduce_scatter(g_one, g_two, extra):
    rows = [g.shape[0] // 32 for g in (g_one, g_two)]
    cols = [g.shape[1] for g in (g_one, g_two)]
    vmem = pl.BlockSpec(memory_space=pltpu.VMEM)
    return pl.pallas_call(
        scatter_kernel,
        out_shape=[jax.ShapeDtypeStruct((r, n), WIDE) for r, n in zip(rows, cols)]
        + [jax.ShapeDtypeStruct(extra.shape, WIDE)],
        in_specs=[vmem] * 3,
        out_specs=[vmem] * 3,
        scratch_shapes=scatter_scratch(rows[0], cols[0]) + scatter_scratch(rows[1], cols[1])
        + [pltpu.VMEM((12,) + extra.shape, WIDE), pltpu.SemaphoreType.DMA((2, 6, 4, 2)),
           pltpu.SemaphoreType.DMA((2, 6))],
        compiler_params=pltpu.CompilerParams(
            collective_id=1, has_side_effects=True, vmem_limit_bytes=48 * 2**20),
    )(g_one.reshape(GRID + (rows[0], cols[0])), g_two.reshape(GRID + (rows[1], cols[1])), extra)


HALF_COLS = 128


def net_scratch(nodes, halo, pixels, width, hidden, kept):
    near = nodes + 2 * halo
    return dict(
        owner_hot=pltpu.VMEM((nodes, pixels), LOW),
        node_hot=pltpu.VMEM((nodes, pixels), LOW),
        bias=pltpu.VMEM((near, nodes), WIDE),
        send_hot=pltpu.VMEM((2 * halo, nodes), LOW),
        inv_count=pltpu.VMEM((nodes, 1), WIDE),
        sums=pltpu.VMEM((2 * nodes, 2 * HALF_COLS), LOW),
        wave=pltpu.VMEM((2, 4, width), WIDE),
        d_wave=pltpu.VMEM((2, 4, width), WIDE),
        start=pltpu.VMEM((nodes, width), WIDE),
        unit_one=pltpu.VMEM((2, nodes, width), LOW),
        inv_one=pltpu.VMEM((2, nodes, 1), WIDE),
        normed=pltpu.VMEM((2 * near, width), LOW),
        queries=pltpu.VMEM((2, nodes, width), LOW),
        extended=pltpu.VMEM((2, near, 2 * width), LOW),
        probs=pltpu.VMEM((2, HEADS, near, nodes), LOW),
        mixed=pltpu.VMEM((2 * nodes, width), LOW),
        unit_two=pltpu.VMEM((2, nodes, width), LOW),
        inv_two=pltpu.VMEM((2, nodes, 1), WIDE),
        second=pltpu.VMEM((2 * nodes, width), LOW),
        gated=pltpu.VMEM((2 * nodes, hidden), LOW),
        slope=pltpu.VMEM((2 * nodes, hidden), LOW),
        final=pltpu.VMEM((2 * nodes, width), LOW),
        taken=pltpu.VMEM((2 * nodes, HALF_COLS), LOW),
        d_branch=pltpu.VMEM((2 * nodes, width), LOW),
        d_attn=pltpu.VMEM((2 * nodes, width), LOW),
        d_queries=pltpu.VMEM((2 * nodes, width), LOW),
        d_keyval=pltpu.VMEM((2 * near, 2 * width), LOW),
        d_summed=pltpu.VMEM((2 * nodes, width), LOW),
        d_mixed=pltpu.VMEM((nodes, width), LOW),
        d_scores=pltpu.VMEM((near, nodes), LOW),
        scores=pltpu.VMEM((near, nodes), WIDE),
        d_normed=pltpu.VMEM((nodes, width), WIDE),
        outgoing=pltpu.VMEM((4, 2 * halo, width), LOW),
        returned=pltpu.VMEM((2, 2 * halo, width), LOW),
        state=pltpu.VMEM((kept, pixels), WIDE),
        aim=pltpu.VMEM((kept, pixels), WIDE),
        extra=pltpu.VMEM((kept, pixels), WIDE),
        low_state=pltpu.VMEM((HALF_COLS, pixels), LOW),
        staged=pltpu.VMEM((2, 256, hidden), LOW),
        w_early=pltpu.VMEM(GRID + (width // 32, 5 * width), LOW),
        w_up=pltpu.VMEM(GRID + (width // 32, hidden), LOW),
        w_down=pltpu.VMEM(GRID + (hidden // 32, width), LOW),
        loads=pltpu.SemaphoreType.DMA((7,)),
        stores=pltpu.SemaphoreType.DMA((2,)),
        links=pltpu.SemaphoreType.DMA((2, 4, 2)),
        spread=pltpu.SemaphoreType.DMA((2, 6, 4, 3)),
    )


def loop(count, body):
    def step(i, carry):
        body(i)
        return carry

    lax.fori_loop(0, count, step, 0)


def block(index, size):
    return pl.ds(pl.multiple_of(index * size, size), size)


def spread_steps(arrays, sems, first, where):
    z, y, x, c, sibling, across_x, across_y, along_z = where
    planes, x_one, y_one, x_two, y_two, core = {}, {}, {}, {}, {}, {}

    def plane_of(d):
        return (z - d + 4) % 4

    def cross(d):
        for i, out in enumerate(arrays):
            h = out.shape[-1] // 2
            here_l, here_r = out.at[plane_of(d), y, x, c, :, :h], out.at[plane_of(d), y, x, c, :, h:]
            x_one[d, i] = send(here_l, here_l, sems, (1, d, first + i), across_x)
            y_one[d, i] = send(here_r, here_r, sems, (2, d, first + i), across_y)

    def begin():
        for i, out in enumerate(arrays):
            mine = out.at[z, y, x, c]
            for d in (1, 3, 2):
                planes[d, i] = send(mine, mine, sems, (0, d, first + i), along_z[d])
        cross(0)

    def arrive(d):
        for i in range(len(arrays)):
            planes[d, i].wait_recv()
        cross(d)

    def turn(d):
        for i, out in enumerate(arrays):
            h = out.shape[-1] // 2
            x_one[d, i].wait_recv()
            both = out.at[plane_of(d), y, :, c, :, :h]
            y_two[d, i] = send(both, both, sems, (3, d, first + i), across_y)
            y_one[d, i].wait_recv()
            both = out.at[plane_of(d), :, x, c, :, h:]
            x_two[d, i] = send(both, both, sems, (4, d, first + i), across_x)

    def share(d):
        for i, out in enumerate(arrays):
            y_two[d, i].wait_recv()
            x_two[d, i].wait_recv()
            plane = out.at[plane_of(d), :, :, c]
            core[d, i] = send(plane, plane, sems, (5, d, first + i), sibling)

    def end():
        for group in (planes, x_one, y_one, x_two, y_two):
            for copy in group.values():
                copy.wait_send()
        for copy in core.values():
            copy.wait()

    do = functools.partial
    return [begin, do(arrive, 1), do(arrive, 3), do(turn, 0), do(arrive, 2), do(turn, 1), do(turn, 3), do(share, 0),
            do(turn, 2), do(share, 1), do(share, 3), do(share, 2), end]


def net_kernel(names, chan, gathered, numbers, counts, previous, noisy, target, noise, owners, decode_idx, near_idx,
               send_idx, waves, *rest):
    weights, (g_wide, g_down, loss), scratch = rest[: len(rest) - 3 - len(names)], rest[-3 - len(names) : -len(names)], rest[-len(names) :]
    r = types.SimpleNamespace(**dict(zip(names, scratch)))
    nodes, pixels = near_idx.shape[1], owners.shape[1]
    halo = send_idx.shape[0] // 2
    near = nodes + 2 * halo
    width, hidden = r.start.shape[1], r.gated.shape[1]
    at = [0, 3 * width, 4 * width, 4 * width + hidden, 4 * width + hidden + 256, 4 * width + hidden + 384]
    tile = 1024
    tiles = pixels // tile
    patches = lax.axis_size("patch")
    me = lax.axis_index("patch")
    lower, upper = {"patch": (me + patches - 1) % patches}, {"patch": (me + 1) % patches}
    barrier = pltpu.get_barrier_semaphore()
    others = [lower, upper]
    if not gathered:
        where = places()
        z, y, x, c, sibling, across_x, across_y, along_z = where
        others += [sibling, across_x, across_y] + along_z[1:]
    for other in others:
        pl.semaphore_signal(barrier, inc=1, device_id=other, device_id_type=MESH)

    def load(src, dst, slot):
        copy = pltpu.make_async_copy(src, dst, r.loads.at[slot])
        copy.start()
        return copy

    pairs = ((previous, r.low_state), (noisy, r.state), (target, r.aim), (noise, r.extra))
    loads = [load(src, dst, slot) for slot, (src, dst) in enumerate(pairs)]
    rows_used = r.state.shape[0]
    w_at = [0, width, 3 * width, 4 * width, 4 * width + HALF_COLS, 4 * width + 2 * HALF_COLS, 4 * width + 3 * HALF_COLS]
    w_targets = (r.w_early, r.w_up, r.w_down)
    early_steps, late_steps = [], []
    if gathered:
        pl.semaphore_wait(barrier, len(others))
        for i, (src, dst) in enumerate(zip(weights, w_targets)):
            load(src, dst, 4 + i).wait()
    else:
        project, output, encode_prev, encode_noisy, decode, noise_rows, up, down = weights
        r.w_early[z, y, x, c, :, 4 * width :] = jnp.zeros((width // 32, width), LOW)
        for i, piece in ((0, project), (2, output), (3, encode_prev), (4, encode_noisy), (5, decode), (6, noise_rows)):
            r.w_early[z, y, x, c, :, w_at[i] : w_at[i] + piece.shape[1]] = piece[...].astype(LOW)
        r.w_up[z, y, x, c] = up[...].astype(LOW)
        r.w_down[z, y, x, c] = down[...].astype(LOW)
        early_steps = spread_steps(w_targets[:1], r.spread, 0, where)
        late_steps = spread_steps(w_targets[1:], r.spread, 1, where)
        pl.semaphore_wait(barrier, len(others))

    def advance(steps, count):
        for _ in range(min(count, len(steps))):
            steps.pop(0)()

    def early(first, last):
        return r.w_early[:, :, :, :, :, w_at[first] : (w_at + [5 * width])[last]].reshape(width, -1)

    def all_up():
        return r.w_up[...].reshape(width, hidden)

    advance(early_steps, 1)

    level = [numbers[4 * s] for s in range(2)]
    c_in = [numbers[4 * s + 1] for s in range(2)]
    c_skip = [numbers[4 * s + 2] for s in range(2)]
    c_out = [numbers[4 * s + 3] for s in range(2)]

    def build_hot(t):
        cols = block(t, tile)
        place = lax.broadcasted_iota(jnp.int32, (1, tile), 1) + t * tile
        own = jnp.where(place < counts[1], owners[:, cols], -1)
        three = [decode_idx[i : i + 1, cols] for i in range(3)]

        def rows(b):
            row = lax.broadcasted_iota(jnp.int32, (16, tile), 0) + b * 16
            r.owner_hot[block(b, 16), cols] = (row == own).astype(WIDE).astype(LOW)
            total = sum((row == idx).astype(WIDE) for idx in three)
            r.node_hot[block(b, 16), cols] = total.astype(LOW)

        loop(nodes // 16, rows)


    def build_bias(b):
        rows = block(b, 32)
        place = lax.broadcasted_iota(jnp.int32, (32, nodes), 0) + b * 32
        listed = jnp.zeros((32, nodes), WIDE)
        for j in range(1, NEIGH):
            listed = listed + (near_idx[j : j + 1] == place).astype(WIDE)
        listed = jnp.where((place >= nodes) | (place < counts[0]), listed, 0.0)
        listed = listed + (near_idx[0:1] == place).astype(WIDE)
        r.bias[rows] = jnp.where(listed > 0.0, jnp.log(jnp.maximum(listed, 1.0)), -1e30)

    loop(near // 32, build_bias)
    advance(early_steps, 4)
    advance(late_steps, 1)
    for t in range(tiles):
        build_hot(t)
        advance(early_steps, 2)
    r.send_hot[...] = (
        lax.broadcasted_iota(jnp.int32, (2 * halo, nodes), 1) == send_idx[...]
    ).astype(WIDE).astype(LOW)

    loads[0].wait()
    summed = nt(r.owner_hot[...], r.low_state[...])
    channel = lax.broadcasted_iota(jnp.int32, (nodes, HALF_COLS), 1)
    total = jnp.sum(jnp.where(channel == chan, summed, 0.0), axis=1, keepdims=True)
    r.inv_count[...] = 1.0 / jnp.maximum(total, 1.0)
    summed = jnp.where(channel < chan, summed, 0.0).astype(LOW)
    r.sums[:nodes, :HALF_COLS] = summed
    r.sums[nodes:, :HALF_COLS] = summed
    for copy in loads[1:]:
        copy.wait()
    r.low_state[:rows_used] = (r.state[...] * c_in[0]).astype(LOW)
    r.sums[:nodes, HALF_COLS:] = nt(r.owner_hot[...], r.low_state[...]).astype(LOW)
    advance(early_steps, len(early_steps))
    advance(late_steps, 3)

    noise_block = early(6, 7).astype(WIDE).reshape(32, 16, 128)
    lane = lax.broadcasted_iota(jnp.int32, (1, 128), 1)
    for s in range(2):
        parts = jnp.sum(noise_block * waves[s][None], axis=1)
        both = parts + pltpu.roll(parts, 64, 1)
        for k in range(16):
            piece = jnp.where(lane < 64, both[2 * k : 2 * k + 1], both[2 * k + 1 : 2 * k + 2])
            r.wave[s, k // 4 : k // 4 + 1, (k % 4) * 128 : (k % 4 + 1) * 128] = piece


    def pass_on(number, first, second):
        copies = []
        for i, (dst, device) in enumerate(((first, lower), (second, upper))):
            copy = pltpu.make_async_remote_copy(
                src_ref=r.outgoing.at[number, i * halo : (i + 1) * halo], dst_ref=dst,
                send_sem=r.links.at[0, number, i], recv_sem=r.links.at[1, number, i],
                device_id=device, device_id_type=MESH,
            )
            copy.start()
            copies.append(copy)
        return copies

    def encode(s):
        rows = slice(s * nodes, (s + 1) * nodes)
        if s:
            r.low_state[:rows_used] = (r.state[...] * c_in[s]).astype(LOW)
            r.sums[rows, HALF_COLS:] = nt(r.owner_hot[...], r.low_state[...]).astype(LOW)
        r.start[...] = nt(r.sums[rows], early(3, 5)) * r.inv_count[...]

        def norm(b):
            part = block(b, 64)
            unit, inverse = norm_parts(r.start[part])
            r.unit_one[s, part] = unit.astype(LOW)
            r.inv_one[s, part] = inverse
            scaled = unit * (1.0 + r.wave[s, 0:1]) + r.wave[s, 1:2]
            r.normed[pl.ds(pl.multiple_of(s * nodes + b * 64, 64), 64)] = scaled.astype(LOW)

        loop(nodes // 64, norm)
        normed = r.normed[rows]
        r.outgoing[s] = nn(r.send_hot[...], normed).astype(LOW)
        first = 2 * nodes + 2 * halo * s
        copies = pass_on(s, r.normed.at[first + halo : first + 2 * halo], r.normed.at[first : first + halo])
        r.queries[s] = nn(normed, early(0, 1)).astype(LOW)
        advance(late_steps, 1)
        r.extended[s, :nodes] = nn(normed, early(1, 2)).astype(LOW)
        advance(late_steps, 1)
        return copies

    def attend(s, copies):
        rows = slice(s * nodes, (s + 1) * nodes)
        for copy in copies:
            copy.wait()
        first = 2 * nodes + 2 * halo * s
        r.extended[s, nodes:] = nn(r.normed[first : first + 2 * halo], early(1, 2)).astype(LOW)
        for head in range(HEADS):
            cols = slice(head * HD, (head + 1) * HD)
            r.scores[...] = nt(r.extended[s, :, cols], r.queries[s, :, cols])

            def soft(b):
                part = block(b, 128)
                top = jnp.full((8, 128), -1e30, WIDE)
                for k in range(near // 64):
                    rows = slice(k * 64, (k + 1) * 64)
                    score = r.scores[rows, part] * SCALE + r.bias[rows, part]
                    r.scores[rows, part] = score
                    top = jnp.maximum(top, jnp.max(score.reshape(8, 8, 128), axis=0))
                top = jnp.max(top, axis=0, keepdims=True)
                total = jnp.zeros((8, 128), WIDE)
                for k in range(near // 64):
                    rows = slice(k * 64, (k + 1) * 64)
                    weight = jnp.exp(r.scores[rows, part] - top)
                    r.scores[rows, part] = weight
                    total = total + jnp.sum(weight.reshape(8, 8, 128), axis=0)
                total = 1.0 / jnp.sum(total, axis=0, keepdims=True)
                for k in range(near // 64):
                    rows = slice(k * 64, (k + 1) * 64)
                    r.probs[s, head, rows, part] = (r.scores[rows, part] * total).astype(LOW)

            loop(nodes // 128, soft)
            values = r.extended[s, :, width + head * HD : width + (head + 1) * HD]
            r.mixed[rows, cols] = tn(values, r.probs[s, head]).T.astype(LOW)
            advance(late_steps, 2)
        advance(late_steps, len(late_steps))
        r.start[...] += nn(r.mixed[rows], early(2, 3))

        def norm(b):
            part = block(b, 64)
            unit, inverse = norm_parts(r.start[part])
            r.unit_two[s, part] = unit.astype(LOW)
            r.inv_two[s, part] = inverse
            scaled = unit * (1.0 + r.wave[s, 2:3]) + r.wave[s, 3:4]
            r.second[pl.ds(pl.multiple_of(s * nodes + b * 64, 64), 64)] = scaled.astype(LOW)

        loop(nodes // 64, norm)

        def feed(j):
            cols = block(j, 256)
            upward = nn(r.second[rows], r.w_up[:, :, :, :, :, cols].reshape(width, 256))
            gate = 1.0 / (1.0 + jnp.exp(-upward))
            r.gated[rows, cols] = (upward * gate).astype(LOW)
            r.slope[rows, cols] = (gate * (1.0 + upward * (1.0 - gate))).astype(LOW)

        loop(hidden // 256, feed)
        r.final[rows] = (r.start[...] + nn(r.gated[rows], r.w_down[...].reshape(hidden, width))).astype(LOW)
        out = nn(r.final[rows], early(5, 6)) * (1.0 / 3.0)
        return out.T.astype(LOW)[:rows_used]

    def gradient(s):
        rows = slice(s * nodes, (s + 1) * nodes)
        taken = (nt(r.node_hot[...], r.low_state[...]) * (1.0 / 3.0)).astype(LOW)
        r.taken[rows] = taken
        d_final = nt(taken, early(5, 6))
        r.start[...] = d_final
        r.d_branch[rows] = d_final.astype(LOW)

        def feed(j):
            cols = block(j, 256)
            d_gated = nt(r.d_branch[rows], r.w_down[j // 2, j % 2].reshape(256, width))
            r.slope[rows, cols] = (d_gated * r.slope[rows, cols].astype(WIDE)).astype(LOW)

        loop(hidden // 256, feed)
        r.d_normed[...] = nt(r.slope[rows], all_up())
        norm_gradient(s, r.unit_two, r.inv_two, 2)
        r.d_attn[rows] = r.start[...].astype(LOW)
        r.d_mixed[...] = nt(r.d_attn[rows], early(2, 3)).astype(LOW)
        first = 2 * nodes + 2 * halo * s
        far = slice(first, first + 2 * halo)
        for head in range(HEADS):
            cols = slice(head * HD, (head + 1) * HD)
            after = slice(width + head * HD, width + (head + 1) * HD)
            r.scores[...] = nt(r.extended[s, :, after], r.d_mixed[:, cols])

            def soft(b):
                part = block(b, 128)
                total = jnp.zeros((8, 128), WIDE)
                for k in range(near // 64):
                    rows = slice(k * 64, (k + 1) * 64)
                    slope = r.probs[s, head, rows, part].astype(WIDE) * r.scores[rows, part]
                    total = total + jnp.sum(slope.reshape(8, 8, 128), axis=0)
                total = jnp.sum(total, axis=0, keepdims=True)
                for k in range(near // 64):
                    rows = slice(k * 64, (k + 1) * 64)
                    slope = r.probs[s, head, rows, part].astype(WIDE) * (r.scores[rows, part] - total)
                    r.d_scores[rows, part] = (slope * SCALE).astype(LOW)

            loop(nodes // 128, soft)
            d_values = nn(r.probs[s, head], r.d_mixed[:, cols]).astype(LOW)
            d_keys = nn(r.d_scores[...], r.queries[s, :, cols]).astype(LOW)
            r.d_keyval[rows, after] = d_values[:nodes]
            r.d_keyval[far, after] = d_values[nodes:]
            r.d_keyval[rows, cols] = d_keys[:nodes]
            r.d_keyval[far, cols] = d_keys[nodes:]
            r.d_queries[rows, cols] = tn(r.extended[s, :, cols], r.d_scores[...]).T.astype(LOW)
        r.outgoing[2 + s] = nt(r.d_keyval[far], early(1, 2)).astype(LOW)
        copies = pass_on(2 + s, r.returned.at[s, halo:], r.returned.at[s, :halo])
        r.d_normed[...] = nt(r.d_queries[rows], early(0, 1)) + nt(r.d_keyval[rows], early(1, 2))
        return copies

    def norm_gradient(s, units, inverses, which):
        r.d_wave[s, which : which + 2] = jnp.zeros((2, width), WIDE)

        def norm(b):
            part = block(b, 64)
            unit = units[s, part].astype(WIDE)
            d_out = r.d_normed[part]
            d_scale = jnp.sum(d_out * unit, axis=0, keepdims=True)
            d_shift = jnp.sum(d_out, axis=0, keepdims=True)
            r.d_wave[s, which : which + 1] += d_scale
            r.d_wave[s, which + 1 : which + 2] += d_shift
            d_unit = d_out * (1.0 + r.wave[s, which : which + 1])
            along = jnp.mean(d_unit * unit, axis=-1, keepdims=True)
            d_hidden = d_unit - jnp.mean(d_unit, axis=-1, keepdims=True) - unit * along
            r.start[part] += inverses[s, part] * d_hidden

        loop(nodes // 64, norm)

    def absorb(s, copies):
        rows = slice(s * nodes, (s + 1) * nodes)
        for copy in copies:
            copy.wait()
        r.d_normed[...] += tn(r.send_hot[...], r.returned[s])
        norm_gradient(s, r.unit_one, r.inv_one, 0)
        r.d_summed[rows] = (r.start[...] * r.inv_count[...]).astype(LOW)

    copies = encode(0)
    nodes_out = attend(0, copies)

    def decode_one(t):
        cols = block(t, tile)
        out = nn(nodes_out, r.node_hot[:, cols])
        r.state[:, cols] = c_skip[0] * r.state[:, cols] + c_out[0] * out + level[1] * r.extra[:, cols]

    loop(tiles, decode_one)
    copies = encode(1)
    nodes_out_two = attend(1, copies)
    loss[...] = jnp.zeros(loss.shape, WIDE)

    def decode_two(t):
        cols = block(t, tile)
        out = nn(nodes_out_two, r.node_hot[:, cols])
        place = lax.broadcasted_iota(jnp.int32, (1, tile), 1) + t * tile
        error = c_skip[1] * r.state[:, cols] + c_out[1] * out - r.aim[:, cols]
        error = jnp.where(place < counts[1], error, 0.0)
        loss[...] += jnp.sum(error * error)
        r.extra[:, cols] = 2.0 * error
        r.low_state[:rows_used, cols] = (c_out[1] * 2.0 * error).astype(LOW)

    loop(tiles, decode_two)
    copies = gradient(1)
    absorb(1, copies)
    d_nodes = nn(r.d_summed[nodes:], early(4, 5))
    d_nodes = d_nodes.T.astype(LOW)[:rows_used]

    def into_one(t):
        cols = block(t, tile)
        d_noisy = c_skip[1] * r.extra[:, cols] + c_in[1] * nn(d_nodes, r.owner_hot[:, cols])
        r.low_state[:rows_used, cols] = (c_out[0] * d_noisy).astype(LOW)

    loop(tiles, into_one)
    copies = gradient(0)

    stores = [None, None]

    def store(slot, dst, cols):
        copy = pltpu.make_async_copy(r.staged.at[slot, :, :cols], dst, r.stores.at[slot])
        copy.start()
        stores[slot] = copy

    done = [0]

    def product(left, i, right, out, first):
        slot, cols = done[0] % 2, right.shape[1]
        done[0] += 1
        if stores[slot] is not None:
            stores[slot].wait()
        r.staged[slot, :, :cols] = tn(left[:, i * 256 : (i + 1) * 256], right[...]).astype(LOW)
        store(slot, out.at[i * 256 : (i + 1) * 256, first : first + cols], cols)

    for i in range(hidden // 256):
        product(r.gated, i, r.d_branch, g_down, 0)
    for i in range(width // 256):
        product(r.second, i, r.slope, g_wide, at[2])
        product(r.mixed, i, r.d_attn, g_wide, at[1])
        product(r.final, i, r.taken, g_wide, at[4])
        product(r.normed, i, r.d_keyval, g_wide, width)
        product(r.normed.at[: 2 * nodes], i, r.d_queries, g_wide, 0)
    absorb(0, copies)
    for i in range(width // 256):
        product(r.d_summed, i, r.sums, g_wide, at[3])
    for i in range(2):
        slot = (done[0] + i) % 2
        stores[slot].wait()
        total = jnp.zeros((16, 16, 128), WIDE)
        for s in range(2):
            pieces = []
            for k in range(8 * i, 8 * i + 8):
                piece = r.d_wave[s, k // 4 : k // 4 + 1, (k % 4) * 128 : (k % 4 + 1) * 128]
                turned = pltpu.roll(piece, 64, 1)
                pieces.append(jnp.where(lane < 64, piece, turned))
                pieces.append(jnp.where(lane < 64, turned, piece))
            rows = jnp.concatenate(pieces, axis=0)
            total = total + rows[:, None, :] * waves[s][None]
        r.staged[slot, :, :128] = total.reshape(256, 128).astype(LOW)
        store(slot, g_wide.at[i * 256 : (i + 1) * 256, at[5] : at[5] + 128], 128)
    for copy in stores:
        copy.wait()


def run_net(chan, gathered, numbers, counts, previous, noisy, target, noise, owners, decode_idx, near_idx, send_idx,
            waves, width, hidden, weights):
    nodes, pixels = near_idx.shape[1], owners.shape[1]
    scratch = net_scratch(nodes, send_idx.shape[0] // 2, pixels, width, hidden, noisy.shape[0])
    vmem, smem = pl.BlockSpec(memory_space=pltpu.VMEM), pl.BlockSpec(memory_space=pltpu.SMEM)
    hbm = pl.BlockSpec(memory_space=pl.ANY)
    wide = 4 * width + hidden + 4 * HALF_COLS
    return pl.pallas_call(
        functools.partial(net_kernel, tuple(scratch), chan, gathered),
        out_shape=[jax.ShapeDtypeStruct((width, wide), LOW), jax.ShapeDtypeStruct((hidden, width), LOW),
                   jax.ShapeDtypeStruct((8, 128), WIDE)],
        in_specs=[smem] * 2 + [hbm] * 4 + [vmem] * 5 + [hbm if gathered else vmem] * len(weights),
        out_specs=[hbm, hbm, vmem],
        scratch_shapes=list(scratch.values()),
        compiler_params=pltpu.CompilerParams(
            collective_id=3, has_side_effects=True, vmem_limit_bytes=VMEM_LIMIT),
    )(numbers, counts, previous, noisy, target, noise, owners, decode_idx, near_idx, send_idx, waves, *weights)


def fill(array, columns):
    return jnp.pad(array, ((0, 0), (0, columns - array.shape[1])))


def on_device(
    previous_state, target_state, noise_draws, noise_level, pixel_owner, mesh_to_grid, neighbours, halo_send,
    node_count, pixel_count, w_encode, w_project, w_output, w_up, w_down, w_noise, w_decode,
    m_encode, m_project, m_output, m_up, m_down, m_noise, m_decode,
    v_encode, v_project, v_output, v_up, v_down, v_noise, v_decode,
):
    width = w_project.shape[1] // 3
    hidden = w_up.shape[1]
    channels = previous_state.shape[1]
    rows = w_project.shape[0]
    small_slice = lax.axis_size("patch") == 8 and lax.axis_size("rep") == 4
    flipped = w_encode.T
    halves = (flipped[:, :channels], flipped[:, channels:])
    if small_slice:
        weights = (w_project, w_output) + halves + (w_decode, w_noise.reshape(rows, HALF_COLS), w_up, w_down)
    else:
        pieces = [w_project, w_output] + [fill(half, HALF_COLS) for half in halves] + [fill(w_decode, HALF_COLS)]
        early = lax.all_gather(jnp.concatenate(pieces, axis=1).astype(LOW), BOTH, axis=0, tiled=True)
        noise = lax.all_gather(w_noise.astype(LOW), BOTH, axis=1, tiled=True).reshape(FOUR, -1, 64)
        early = jnp.concatenate([early, noise.transpose(1, 0, 2).reshape(width, HALF_COLS)], axis=1)
        all_up = lax.all_gather(w_up.astype(LOW), BOTH, axis=0, tiled=True)
        all_down = lax.all_gather(w_down.astype(LOW), BOTH, axis=0, tiled=True)
        weights = [w.reshape(GRID + (-1, w.shape[1])) for w in (early, all_up, all_down)]
    at = [0, 3 * width, 4 * width, 4 * width + hidden, 4 * width + hidden + 256, 4 * width + hidden + 384]

    levels = noise_level[0]
    pixels = pixel_owner.shape[1]
    padding = ((0, -channels % 16), (0, 0))
    previous = jnp.concatenate([previous_state[0], jnp.ones((1, pixels), WIDE)], axis=0).astype(LOW)
    previous = jnp.pad(previous, ((0, HALF_COLS - channels - 1), (0, 0)))
    target = jnp.pad(target_state[0], padding)
    noisy = jnp.pad(target_state[0] + levels[0] * noise_draws[0, 0], padding)
    noise_two = jnp.pad(noise_draws[0, 1], padding)
    c_in = lax.rsqrt(levels * levels + 1.0)
    numbers = jnp.stack([levels, c_in, 1.0 / (levels * levels + 1.0), levels * c_in], axis=1).reshape(8)
    counts = jnp.concatenate([node_count[0], pixel_count[0]])
    waves = jnp.stack([fourier(levels[i]).reshape(FOUR // 2, 2) for i in range(2)])
    waves = jnp.repeat(waves, 64, axis=2)
    g_wide, g_down, loss_local = run_net(
        channels, not small_slice, numbers, counts, previous, noisy, target, noise_two, pixel_owner, mesh_to_grid[0],
        neighbours[0].T, halo_send.reshape(-1, 1), waves, width, hidden, weights,
    )
    count_local = (channels * jnp.minimum(pixel_count[0, 0], pixels)).astype(WIDE)
    if small_slice:
        row = lax.broadcasted_iota(jnp.int32, (8, 128), 0)
        extra = jnp.where(row == 1, loss_local, 0.0) + jnp.where(row == 2, count_local, 0.0)
        s_wide, s_down, totals = reduce_scatter(g_wide, g_down, extra)
        totals = totals[:3, 0]
        s_noise = s_wide[:, at[5] :].reshape(FOUR, -1)
    else:
        g_noise = g_wide[:, at[5] :].reshape(-1, FOUR, 64).transpose(1, 0, 2).reshape(FOUR, -1)
        s_wide = lax.psum_scatter(g_wide[:, : at[5]].astype(WIDE), BOTH, scatter_dimension=0, tiled=True)
        s_down = lax.psum_scatter(g_down.astype(WIDE), BOTH, scatter_dimension=0, tiled=True)
        s_noise = lax.psum_scatter(g_noise.astype(WIDE), BOTH, scatter_dimension=1, tiled=True)
        squares = jnp.sum(s_wide * s_wide) + jnp.sum(s_down * s_down) + jnp.sum(s_noise * s_noise)
        totals = lax.psum((squares, loss_local[0, 0], count_local), BOTH)
    second = at[3] + HALF_COLS
    shards = (
        jnp.concatenate([s_wide[:, at[3] : at[3] + channels], s_wide[:, second : second + channels]], axis=1).T,
        s_wide[:, : at[1]],
        s_wide[:, at[1] : at[2]],
        s_wide[:, at[2] : at[3]],
        s_down,
        s_noise,
        s_wide[:, at[4] : at[4] + channels],
    )
    grad_norm = jnp.sqrt(totals[0])
    factor = THRESHOLD / jnp.maximum(grad_norm, THRESHOLD)
    masters = (w_encode, w_project, w_output, w_up, w_down, w_noise, w_decode)
    moments = (m_encode, m_project, m_output, m_up, m_down, m_noise, m_decode)
    seconds = (v_encode, v_project, v_output, v_up, v_down, v_noise, v_decode)
    new_weights, new_moments, new_seconds = ([], [], [])
    for w, m, v, g in zip(masters, moments, seconds, shards):
        clipped = g * factor
        moment = BETA_ONE * m + (1.0 - BETA_ONE) * clipped
        variance = BETA_TWO * v + (1.0 - BETA_TWO) * clipped * clipped
        stepped = (
            moment
            / (1.0 - BETA_ONE**STEP)
            / (jnp.sqrt(variance / (1.0 - BETA_TWO**STEP)) + EPSILON)
        )
        new_weights.append(w - LEARN_RATE * (stepped + DECAY_RATE * w))
        new_moments.append(moment)
        new_seconds.append(variance)
    return (
        tuple(new_weights)
        + tuple(new_moments)
        + tuple(new_seconds)
        + (totals[1], totals[2], grad_norm)
    )


def solution(mesh):
    in_specs = (
        P("rep", None, "patch"),
        P("rep", None, "patch"),
        P("rep", None, None, "patch"),
        P("rep", None),
        P("rep", "patch"),
        P("rep", None, "patch"),
        P("rep", "patch", None),
        P("rep", "patch"),
        P("rep", "patch"),
        P("rep", "patch"),
        P(None, ("patch", "rep")),
        P(("patch", "rep"), None),
        P(("patch", "rep"), None),
        P(("patch", "rep"), None),
        P(("patch", "rep"), None),
        P(None, ("patch", "rep")),
        P(("patch", "rep"), None),
        P(None, ("patch", "rep")),
        P(("patch", "rep"), None),
        P(("patch", "rep"), None),
        P(("patch", "rep"), None),
        P(("patch", "rep"), None),
        P(None, ("patch", "rep")),
        P(("patch", "rep"), None),
        P(None, ("patch", "rep")),
        P(("patch", "rep"), None),
        P(("patch", "rep"), None),
        P(("patch", "rep"), None),
        P(("patch", "rep"), None),
        P(None, ("patch", "rep")),
        P(("patch", "rep"), None),
    )
    out_specs = (
        P(None, ("patch", "rep")),
        P(("patch", "rep"), None),
        P(("patch", "rep"), None),
        P(("patch", "rep"), None),
        P(("patch", "rep"), None),
        P(None, ("patch", "rep")),
        P(("patch", "rep"), None),
        P(None, ("patch", "rep")),
        P(("patch", "rep"), None),
        P(("patch", "rep"), None),
        P(("patch", "rep"), None),
        P(("patch", "rep"), None),
        P(None, ("patch", "rep")),
        P(("patch", "rep"), None),
        P(None, ("patch", "rep")),
        P(("patch", "rep"), None),
        P(("patch", "rep"), None),
        P(("patch", "rep"), None),
        P(("patch", "rep"), None),
        P(None, ("patch", "rep")),
        P(("patch", "rep"), None),
        P(),
        P(),
        P(),
    )
    return jax.shard_map(
        on_device, mesh=mesh, in_specs=in_specs, out_specs=out_specs, check_vma=False
    )
```

profile of v0, /device:TPU:0, one launch (start us, length us, event | category | flops | bytes accessed | tf_op | source)
XLA Modules:
  0.0 223.4 jit_solution(244824880464193664)
XLA Ops:
  0.7 1.3 fusion.29
  2.7 0.1 pad_maximum_fusion.2
  2.8 0.1 stack_reshape.6
  3.6 0.1 pad_maximum_fusion.3
  3.7 0.1 stack_reshape.7
  3.8 0.1 broadcast_in_dim.16
  3.9 0.7 reshape.128.waves
  4.6 0.7 fusion.18
  5.3 0.7 pad_maximum_fusion.1
  5.9 0.1 copy.73
  6.0 0.6 reshape.126.numbers
  6.6 4.1 %fusion.26 = (f32[1,1,84,3072]{3,1,2,0:T(1,128)S(1)}, f32[1,1,84,3072]{3,1,2,0:T(1,128)S(1)}) fusion(f32[1,2,84,3072]{3,1,2,0:T(2,128)} %param.33), kind=kLoop, calls=%fused_computation.64 | loop fusion | bytes 4128768 | tf_op jit(solution)/shard_map/slice | solution.py:757
  10.7 1.0 fusion.2
  11.7 1.2 pad.17.noisy
  12.9 0.2 copy.95
  13.1 0.0 copy-start.14
  13.1 1.2 pad.19.noise
  14.2 0.7 fusion.27
  16.2 0.6 pad_add_fusion.counts
  16.8 0.2 copy.96
  17.0 0.0 copy-start.2
  17.0 1.2 pad.18.target
  18.2 0.4 copy-done.2
  18.6 0.2 copy.97
  18.8 1.0 fusion.previous
  19.8 0.7 copy.77.send_idx
  20.5 0.6 copy.98
  21.1 0.7 reshape.129.rest_5_
  21.8 134.6 %shard_map.478 = (bf16[512,4608]{1,0:T(8,128)(2,1)}, bf16[2048,512]{1,0:T(8,128)(2,1)}, f32[8,128]{1,0:T(8,128)}) custom-call(f32[8]{0:T(128)} %reshape.126.numbers, s32[2]{0:T(128)} %pad_add_fusion.counts, bf16[128,3072]{1,0:T(8,128)(2,1)} %fusion.previous, f32[96,3072]{1,0:T(8,128)} %pad.17.noisy, f32[96,3072]{1,0:T(8,128)} %pad.18.target, ...), custom_call_target="tpu_custom_call" | custom-call | tf_op jit(solution)/shard_map/pallas_call | solution.py:709
  156.5 0.7 select_add_fusion.extra
  157.2 1.6 copy-done
  158.8 0.0 copy-start.8
  158.8 56.7 %shard_map.479 = (f32[16,4608]{1,0:T(8,128)S(1)}, f32[64,512]{1,0:T(8,128)S(1)}, f32[8,128]{1,0:T(8,128)S(1)}) custom-call(bf16[4,2,2,2,16,4608]{5,4,3,2,1,0:T(8,128)(2,1)} %bitcast.50, bf16[4,2,2,2,64,512]{5,4,3,2,1,0:T(8,128)(2,1)S(1)} %bitcast.49, f32[8,128]{1,0:T(8,128)S(1)} %select_add_fusion.extra), custom_call_target="tpu_custom_call" | custom-call | tf_op jit(solution)/shard_map/pallas_call | solution.py:182
  215.6 0.0 copy-start.4
  215.6 0.0 copy-start.9
  215.6 0.0 copy-start.10
  215.6 0.0 copy-start.18
  215.6 0.0 copy-start.5
  215.7 0.5 fusion.28
  216.9 0.1 mul.419
  217.0 0.6 multiply_subtract_fusion.4
  217.7 0.0 copy-start.24
  217.7 0.8 multiply_subtract_fusion
  218.5 0.8 multiply_subtract_fusion.1
  219.3 0.7 multiply_subtract_fusion.3
  220.0 0.8 multiply_subtract_fusion.2
  220.8 0.6 multiply_subtract_fusion.6
  221.4 0.7 multiply_subtract_fusion.5
  (47 shorter events, 0.2 us)
Async XLA Ops:
  6.6 4.1 %copy-start.1 = (f32[1,84,3072]{2,0,1:T(1,128)S(1)}, f32[1,84,3072]{2,0,1:T(1,128)}, u32[]{:S(2)}) copy-start(f32[1,84,3072]{2,0,1:T(1,128)} %param.32) | copy-start | bytes 3096580
  13.1 1.2 copy-start.14
  17.0 1.6 copy-start.2
  18.6 1.1 copy-start.25
  18.6 1.9 copy-start.15
  18.6 2.5 %copy-start.13 = (f32[32,64]{1,0:T(8,128)S(1)}, f32[32,64]{1,0:T(8,128)}, u32[]{:S(2)}) copy-start(f32[32,64]{1,0:T(8,128)} %param.46) | copy-start | bytes 24580
  157.2 1.6 copy-start
  158.8 58.2 %copy-start.19 = (f32[32,64]{1,0:T(8,128)S(1)}, f32[32,64]{1,0:T(8,128)}, u32[]{:S(2)}) copy-start(f32[32,64]{1,0:T(8,128)} %param.53) | copy-start | bytes 24580
  158.8 58.2 %copy-start.20 = (f32[32,64]{1,0:T(8,128)S(1)}, f32[32,64]{1,0:T(8,128)}, u32[]{:S(2)}) copy-start(f32[32,64]{1,0:T(8,128)} %param.60) | copy-start | bytes 24580
  158.8 58.8 %copy-start.3 = (f32[64,512]{1,0:T(8,128)S(1)}, f32[64,512]{1,0:T(8,128)}, u32[]{:S(2)}) copy-start(f32[64,512]{1,0:T(8,128)} %rest_7_.1) | copy-start | bytes 393220
  158.8 58.8 %copy-start.7 = (f32[64,512]{1,0:T(8,128)S(1)}, f32[64,512]{1,0:T(8,128)}, u32[]{:S(2)}) copy-start(f32[64,512]{1,0:T(8,128)} %param.52) | copy-start | bytes 393220
  158.8 58.8 %copy-start.8 = (f32[64,512]{1,0:T(8,128)S(1)}, f32[64,512]{1,0:T(8,128)}, u32[]{:S(2)}) copy-start(f32[64,512]{1,0:T(8,128)} %param.59) | copy-start | bytes 393220
  215.6 2.9 %copy-start.4 = (f32[16,2048]{1,0:T(8,128)S(1)}, f32[16,2048]{1,0:T(8,128)}, u32[]{:S(2)}) copy-start(f32[16,2048]{1,0:T(8,128)} %rest_6_.1) | copy-start | bytes 393220
  215.6 2.9 %copy-start.9 = (f32[16,2048]{1,0:T(8,128)S(1)}, f32[16,2048]{1,0:T(8,128)}, u32[]{:S(2)}) copy-start(f32[16,2048]{1,0:T(8,128)} %param.51) | copy-start | bytes 393220
  215.6 2.9 %copy-start.10 = (f32[16,2048]{1,0:T(8,128)S(1)}, f32[16,2048]{1,0:T(8,128)}, u32[]{:S(2)}) copy-start(f32[16,2048]{1,0:T(8,128)} %param.58) | copy-start | bytes 393220
  215.6 3.7 %copy-start.6 = (f32[16,512]{1,0:T(8,128)S(1)}, f32[16,512]{1,0:T(8,128)}, u32[]{:S(2)}) copy-start(f32[16,512]{1,0:T(8,128)} %rest_1_.1) | copy-start | bytes 98308
  215.6 3.7 %copy-start.17 = (f32[16,512]{1,0:T(8,128)S(1)}, f32[16,512]{1,0:T(8,128)}, u32[]{:S(2)}) copy-start(f32[16,512]{1,0:T(8,128)} %param.50) | copy-start | bytes 98308
  215.6 3.7 %copy-start.18 = (f32[16,512]{1,0:T(8,128)S(1)}, f32[16,512]{1,0:T(8,128)}, u32[]{:S(2)}) copy-start(f32[16,512]{1,0:T(8,128)} %param.57) | copy-start | bytes 98308
  215.6 4.4 %copy-start.5 = (f32[16,1536]{1,0:T(8,128)S(1)}, f32[16,1536]{1,0:T(8,128)}, u32[]{:S(2)}) copy-start(f32[16,1536]{1,0:T(8,128)} %rest_0_.1) | copy-start | bytes 294916
  215.6 4.4 %copy-start.11 = (f32[16,1536]{1,0:T(8,128)S(1)}, f32[16,1536]{1,0:T(8,128)}, u32[]{:S(2)}) copy-start(f32[16,1536]{1,0:T(8,128)} %param.49) | copy-start | bytes 294916
  215.6 4.3 %copy-start.12 = (f32[16,1536]{1,0:T(8,128)S(1)}, f32[16,1536]{1,0:T(8,128)}, u32[]{:S(2)}) copy-start(f32[16,1536]{1,0:T(8,128)} %param.56) | copy-start | bytes 294916
  217.7 3.1 %copy-start.16 = (f32[16,84]{1,0:T(8,128)S(1)}, f32[16,84]{1,0:T(8,128)}, u32[]{:S(2)}) copy-start(f32[16,84]{1,0:T(8,128)} %rest_4_.1) | copy-start | bytes 16132
  217.7 3.1 %copy-start.23 = (f32[16,84]{1,0:T(8,128)S(1)}, f32[16,84]{1,0:T(8,128)}, u32[]{:S(2)}) copy-start(f32[16,84]{1,0:T(8,128)} %param.54) | copy-start | bytes 16132
  217.7 3.1 %copy-start.24 = (f32[16,84]{1,0:T(8,128)S(1)}, f32[16,84]{1,0:T(8,128)}, u32[]{:S(2)}) copy-start(f32[16,84]{1,0:T(8,128)} %param.61) | copy-start | bytes 16132
  218.5 2.9 %copy-start.21 = (f32[168,16]{0,1:T(8,128)S(1)}, f32[168,16]{0,1:T(8,128)}, u32[]{:S(2)}) copy-start(f32[168,16]{0,1:T(8,128)} %param.48) | copy-start | bytes 32260
  218.5 2.9 %copy-start.22 = (f32[168,16]{0,1:T(8,128)S(1)}, f32[168,16]{0,1:T(8,128)}, u32[]{:S(2)}) copy-start(f32[168,16]{0,1:T(8,128)} %param.55) | copy-start | bytes 32260
where the time goes:
time: 227 us; the launch traced here: 223 us
  Pallas kernels  191 us (84%)
  local copies, waits for them, and re-layouts  16.6 us (7%)
  other arithmetic  9.85 us (4%)
  between operations  5.67 us (2%)
    pallas_call x1, Pallas kernels, run_net(): pl.pallas_call(functools.partial(net_kernel, tuple(scratch), chan, gather...  135 us
    pallas_call x1, Pallas kernels, reduce_scatter(): pl.pallas_call(scatter_kernel, out_shape=[jax.ShapeDtypeStruct((r, n), WI...  56.7 us
    sub x7, other arithmetic, on_device(): new_weights.append(w - LEARN_RATE * (stepped + DECAY_RATE * w))  4.99 us

commit v1 on v0

--- a/solution.py
+++ b/solution.py
@@ -26,7 +26,7 @@
 LOW = jnp.bfloat16
 WIDE = jnp.float32
 SCALE = HD ** (-0.5)
-VMEM_LIMIT = 62 * 2**20
+VMEM_LIMIT = 64 * 2**20
 
 
 def nn(a, b):
@@ -68,13 +68,6 @@
     return z, y, x, c, sibling, across_x, across_y, along_z
 
 
-def greet(others):
-    barrier = pltpu.get_barrier_semaphore()
-    for other in others:
-        pl.semaphore_signal(barrier, inc=1, device_id=other, device_id_type=MESH)
-    pl.semaphore_wait(barrier, len(others))
-
-
 def send(src, dst, sems, index, device):
     copy = pltpu.make_async_remote_copy(
         src_ref=src, dst_ref=dst, send_sem=sems.at[(0,) + index], recv_sem=sems.at[(1,) + index],
@@ -89,108 +82,6 @@
     for term in terms[1:]:
         total = total + term.astype(WIDE)
     return total
-
-
-def scatter_scratch(rows, cols):
-    h = cols // 2
-    return [
-        pltpu.VMEM((4, 2, 2, rows, cols), LOW),
-        pltpu.VMEM((4, 2, 2, rows, cols), LOW),
-        pltpu.VMEM((4, 2, rows, h), LOW),
-        pltpu.VMEM((4, 2, rows, h), LOW),
-        pltpu.VMEM((4, rows, h), LOW),
-        pltpu.VMEM((4, 2, rows, h), LOW),
-        pltpu.VMEM((4, 2, rows, h), LOW),
-        pltpu.VMEM((4, rows, h), LOW),
-        pltpu.VMEM((3, rows, cols), LOW),
-        pltpu.VMEM((3, rows, cols), LOW),
-    ]
-
-
-def scatter_kernel(g_one, g_two, extra, out_one, out_two, totals, *scratch):
-    z, y, x, c, sibling, across_x, across_y, along_z = places()
-    parts = ((g_one, out_one) + scratch[:10], (g_two, out_two) + scratch[10:20])
-    board, sems, small = scratch[20:]
-    greet([sibling, across_x, across_y] + along_z[1:])
-    steps = [(d, (z + d) % 4) for d in (1, 2, 3, 0)]
-    sent, first, left, right, left_two, right_two, last = [], {}, {}, {}, {}, {}, {}
-    for d, zd in steps:
-        for i, (g, out, near, acc, near_l, acc_l, end_l, near_r, acc_r, end_r, going, come) in enumerate(parts):
-            first[d, i] = send(g.at[zd, :, :, 1 - c], near.at[zd], sems, (0, d, i), sibling)
-    for d, zd in steps:
-        for i, (g, out, near, acc, near_l, acc_l, end_l, near_r, acc_r, end_r, going, come) in enumerate(parts):
-            h = g.shape[-1] // 2
-            first[d, i].wait_recv()
-            acc[zd] = plus(g[zd, :, :, c], near[zd]).astype(LOW)
-            left[d, i] = send(acc.at[zd, :, 1 - x, :, :h], near_l.at[zd], sems, (1, d, i), across_x)
-            right[d, i] = send(acc.at[zd, 1 - y, :, :, h:], near_r.at[zd], sems, (2, d, i), across_y)
-    for d, zd in steps:
-        for i, (g, out, near, acc, near_l, acc_l, end_l, near_r, acc_r, end_r, going, come) in enumerate(parts):
-            h = g.shape[-1] // 2
-            left[d, i].wait_recv()
-            acc_l[zd] = plus(acc[zd, :, x, :, :h], near_l[zd]).astype(LOW)
-            left_two[d, i] = send(acc_l.at[zd, 1 - y], end_l.at[zd], sems, (3, d, i), across_y)
-            right[d, i].wait_recv()
-            acc_r[zd] = plus(acc[zd, y, :, :, h:], near_r[zd]).astype(LOW)
-            right_two[d, i] = send(acc_r.at[zd, 1 - x], end_r.at[zd], sems, (4, d, i), across_x)
-    for d, zd in steps:
-        for i, (g, out, near, acc, near_l, acc_l, end_l, near_r, acc_r, end_r, going, come) in enumerate(parts):
-            h = g.shape[-1] // 2
-            left_two[d, i].wait_recv()
-            done_l = plus(acc_l[zd, y], end_l[zd])
-            right_two[d, i].wait_recv()
-            done_r = plus(acc_r[zd, x], end_r[zd])
-            if d == 0:
-                out[:, :h] = done_l
-                out[:, h:] = done_r
-            else:
-                going[d - 1, :, :h] = done_l.astype(LOW)
-                going[d - 1, :, h:] = done_r.astype(LOW)
-                last[d, i] = send(going.at[d - 1], come.at[d - 1], sems, (5, d, i), along_z[d])
-    squares = jnp.zeros((), WIDE)
-    for i, part in enumerate(parts):
-        out, come = part[1], part[11]
-        for d in (1, 2, 3):
-            last[d, i].wait_recv()
-        out[...] = plus(out[...], come[0], come[1], come[2])
-        squares = squares + jnp.sum(out[...] * out[...])
-    row = lax.broadcasted_iota(jnp.int32, extra.shape, 0)
-    board[0] = jnp.where(row == 0, squares, extra[...])
-    more = []
-    for phase, device in enumerate((sibling, across_x, across_y)):
-        copy = send(board.at[phase], board.at[4 + phase], small, (phase,), device)
-        copy.wait_recv()
-        more.append(copy)
-        board[phase + 1] = board[phase] + board[4 + phase]
-    for d in (1, 2, 3):
-        more.append(send(board.at[3], board.at[8 + z], small, (2 + d,), along_z[d]))
-    board[8 + z] = board[3]
-    for d in (1, 2, 3):
-        more[2 + d].wait_recv()
-    totals[...] = board[8] + board[9] + board[10] + board[11]
-    for group in (first, left, right, left_two, right_two, last):
-        for copy in group.values():
-            copy.wait_send()
-    for copy in more:
-        copy.wait_send()
-
-
-def reduce_scatter(g_one, g_two, extra):
-    rows = [g.shape[0] // 32 for g in (g_one, g_two)]
-    cols = [g.shape[1] for g in (g_one, g_two)]
-    vmem = pl.BlockSpec(memory_space=pltpu.VMEM)
-    return pl.pallas_call(
-        scatter_kernel,
-        out_shape=[jax.ShapeDtypeStruct((r, n), WIDE) for r, n in zip(rows, cols)]
-        + [jax.ShapeDtypeStruct(extra.shape, WIDE)],
-        in_specs=[vmem] * 3,
-        out_specs=[vmem] * 3,
-        scratch_shapes=scatter_scratch(rows[0], cols[0]) + scatter_scratch(rows[1], cols[1])
-        + [pltpu.VMEM((12,) + extra.shape, WIDE), pltpu.SemaphoreType.DMA((2, 6, 4, 2)),
-           pltpu.SemaphoreType.DMA((2, 6))],
-        compiler_params=pltpu.CompilerParams(
-            collective_id=1, has_side_effects=True, vmem_limit_bytes=48 * 2**20),
-    )(g_one.reshape(GRID + (rows[0], cols[0])), g_two.reshape(GRID + (rows[1], cols[1])), extra)
 
 
 HALF_COLS = 128
@@ -230,19 +121,23 @@
         d_mixed=pltpu.VMEM((nodes, width), LOW),
         d_scores=pltpu.VMEM((near, nodes), LOW),
         scores=pltpu.VMEM((near, nodes), WIDE),
-        d_normed=pltpu.VMEM((nodes, width), WIDE),
         outgoing=pltpu.VMEM((4, 2 * halo, width), LOW),
         returned=pltpu.VMEM((2, 2 * halo, width), LOW),
         state=pltpu.VMEM((kept, pixels), WIDE),
-        aim=pltpu.VMEM((kept, pixels), WIDE),
         extra=pltpu.VMEM((kept, pixels), WIDE),
         low_state=pltpu.VMEM((HALF_COLS, pixels), LOW),
-        staged=pltpu.VMEM((2, 256, hidden), LOW),
+        g_early=pltpu.VMEM(GRID + (width // 32, 5 * width), LOW),
+        g_up=pltpu.VMEM(GRID + (width // 32, hidden), LOW),
+        g_down=pltpu.VMEM(GRID + (hidden // 32, width), LOW),
+        lost=pltpu.VMEM((8, 128), WIDE),
+        board=pltpu.VMEM((12, 8, 128), WIDE),
         w_early=pltpu.VMEM(GRID + (width // 32, 5 * width), LOW),
         w_up=pltpu.VMEM(GRID + (width // 32, hidden), LOW),
         w_down=pltpu.VMEM(GRID + (hidden // 32, width), LOW),
         loads=pltpu.SemaphoreType.DMA((7,)),
-        stores=pltpu.SemaphoreType.DMA((2,)),
+        ready=pltpu.SemaphoreType.REGULAR((2,)),
+        fold=pltpu.SemaphoreType.DMA((2, 6, 4, 3)),
+        small=pltpu.SemaphoreType.DMA((2, 12)),
         links=pltpu.SemaphoreType.DMA((2, 4, 2)),
         spread=pltpu.SemaphoreType.DMA((2, 6, 4, 3)),
     )
@@ -315,9 +210,89 @@
             do(turn, 2), do(share, 1), do(share, 3), do(share, 2), end]
 
 
+def far_planes(z):
+    return [3 * (1 - z // 2), 2 - z // 2, z + 1 - 2 * (z % 2), z]
+
+
+class Fold:
+    def __init__(self, sources, rooms, outs, sems, first, where):
+        self.sources, self.rooms, self.outs, self.sems, self.first = sources, rooms, outs, sems, first
+        self.z, self.y, self.x, self.c, self.sibling, self.across_x, self.across_y, _ = where
+        self.far = far_planes(self.z)
+        self.near, self.one, self.two, self.last = {}, {}, {}, []
+
+    def start(self, k):
+        p = self.far[k]
+        for i, (g, room) in enumerate(zip(self.sources, self.rooms)):
+            self.near[k, i] = send(
+                g.at[p, :, :, 1 - self.c], room.at[p, :, :, 0], self.sems, (0, k, self.first + i), self.sibling)
+
+    def chip(self, k):
+        p = self.far[k]
+        for i, (g, room) in enumerate(zip(self.sources, self.rooms)):
+            h = g.shape[-1] // 2
+            self.near[k, i].wait_recv()
+            room[p, :, :, 0] = plus(g[p, :, :, self.c], room[p, :, :, 0]).astype(LOW)
+            self.one[k, i, 0] = send(room.at[p, :, 1 - self.x, 0, :, :h], room.at[p, 0, :, 1, :, :h], self.sems,
+                                     (1, k, self.first + i), self.across_x)
+            self.one[k, i, 1] = send(room.at[p, 1 - self.y, :, 0, :, h:], room.at[p, 0, :, 1, :, h:], self.sems,
+                                     (2, k, self.first + i), self.across_y)
+
+    def turn(self, k):
+        p = self.far[k]
+        for i, room in enumerate(self.rooms):
+            h = room.shape[-1] // 2
+            self.one[k, i, 0].wait_recv()
+            room[p, 0, :, 1, :, :h] = plus(room[p, :, self.x, 0, :, :h], room[p, 0, :, 1, :, :h]).astype(LOW)
+            self.two[k, i, 0] = send(room.at[p, 0, 1 - self.y, 1, :, :h], room.at[p, 1, 0, 1, :, :h], self.sems,
+                                     (3, k, self.first + i), self.across_y)
+            self.one[k, i, 1].wait_recv()
+            room[p, 0, :, 1, :, h:] = plus(room[p, self.y, :, 0, :, h:], room[p, 0, :, 1, :, h:]).astype(LOW)
+            self.two[k, i, 1] = send(room.at[p, 0, 1 - self.x, 1, :, h:], room.at[p, 1, 0, 1, :, h:], self.sems,
+                                     (4, k, self.first + i), self.across_x)
+
+    def leave(self, k):
+        p = self.far[k]
+        for i, (room, out) in enumerate(zip(self.rooms, self.outs)):
+            h = room.shape[-1] // 2
+            self.two[k, i, 0].wait_recv()
+            self.two[k, i, 1].wait_recv()
+            left = plus(room[p, 0, self.y, 1, :, :h], room[p, 1, 0, 1, :, :h])
+            right = plus(room[p, 0, self.x, 1, :, h:], room[p, 1, 0, 1, :, h:])
+            if k == 3:
+                out[:, :h] = left
+                out[:, h:] = right
+                continue
+            room[p, 1, 0, 1, :, :h] = left.astype(LOW)
+            room[p, 1, 0, 1, :, h:] = right.astype(LOW)
+            copy = pltpu.make_async_remote_copy(
+                src_ref=room.at[p, 1, 0, 1], dst_ref=room.at[self.z, 1, 1, 1],
+                send_sem=self.sems.at[0, 5, k, self.first + i], recv_sem=self.sems.at[1, 5, self.z, self.first + i],
+                device_id={"patch": p * 2 + self.y, "rep": self.x * 2 + self.c}, device_id_type=MESH,
+            )
+            copy.start()
+            self.last.append(copy)
+
+    def end(self):
+        for i, (room, out) in enumerate(zip(self.rooms, self.outs)):
+            for k in range(3):
+                p = self.far[k]
+                come = room.at[p, 1, 1, 1]
+                pltpu.make_async_remote_copy(
+                    src_ref=come, dst_ref=come, send_sem=self.sems.at[0, 5, k, self.first + i],
+                    recv_sem=self.sems.at[1, 5, p, self.first + i], device_id=self.sibling, device_id_type=MESH,
+                ).wait_recv()
+                out[...] = plus(out[...], room[p, 1, 1, 1])
+
+    def drain(self):
+        for copy in list(self.near.values()) + list(self.one.values()) + list(self.two.values()) + self.last:
+            copy.wait_send()
+
+
 def net_kernel(names, chan, gathered, numbers, counts, previous, noisy, target, noise, owners, decode_idx, near_idx,
                send_idx, waves, *rest):
-    weights, (g_wide, g_down, loss), scratch = rest[: len(rest) - 3 - len(names)], rest[-3 - len(names) : -len(names)], rest[-len(names) :]
+    outs = rest[-4 - len(names) : -len(names)]
+    weights, scratch = rest[: -4 - len(names)], rest[-len(names) :]
     r = types.SimpleNamespace(**dict(zip(names, scratch)))
     nodes, pixels = near_idx.shape[1], owners.shape[1]
     halo = send_idx.shape[0] // 2
@@ -334,7 +309,10 @@
     if not gathered:
         where = places()
         z, y, x, c, sibling, across_x, across_y, along_z = where
-        others += [sibling, across_x, across_y] + along_z[1:]
+        folders = [sibling, across_x, across_y] + along_z[1:]
+        plane_peers = [
+            {"patch": z * 2 + (y + m // 4) % 2, "rep": ((x + m // 2 % 2) % 2) * 2 + (c + m % 2) % 2} for m in range(1, 8)]
+        others += plane_peers + along_z[1:]
     for other in others:
         pl.semaphore_signal(barrier, inc=1, device_id=other, device_id_type=MESH)
 
@@ -343,7 +321,7 @@
         copy.start()
         return copy
 
-    pairs = ((previous, r.low_state), (noisy, r.state), (target, r.aim), (noise, r.extra))
+    pairs = ((previous, r.low_state), (noisy, r.state), (noise, r.extra))
     loads = [load(src, dst, slot) for slot, (src, dst) in enumerate(pairs)]
     rows_used = r.state.shape[0]
     w_at = [0, width, 3 * width, 4 * width, 4 * width + HALF_COLS, 4 * width + 2 * HALF_COLS, 4 * width + 3 * HALF_COLS]
@@ -552,8 +530,12 @@
             r.slope[rows, cols] = (d_gated * r.slope[rows, cols].astype(WIDE)).astype(LOW)
 
         loop(hidden // 256, feed)
-        r.d_normed[...] = nt(r.slope[rows], all_up())
+        r.scores[:nodes, :width] = nt(r.slope[rows], all_up())
+        if s == 0:
+            announce(0)
         norm_gradient(s, r.unit_two, r.inv_two, 2)
+        if s == 0:
+            products_late()
         r.d_attn[rows] = r.start[...].astype(LOW)
         r.d_mixed[...] = nt(r.d_attn[rows], early(2, 3)).astype(LOW)
         first = 2 * nodes + 2 * halo * s
@@ -584,9 +566,11 @@
             r.d_keyval[rows, cols] = d_keys[:nodes]
             r.d_keyval[far, cols] = d_keys[nodes:]
             r.d_queries[rows, cols] = tn(r.extended[s, :, cols], r.d_scores[...]).T.astype(LOW)
+            if s == 0:
+                advance(fold_steps, 2)
         r.outgoing[2 + s] = nt(r.d_keyval[far], early(1, 2)).astype(LOW)
         copies = pass_on(2 + s, r.returned.at[s, halo:], r.returned.at[s, :halo])
-        r.d_normed[...] = nt(r.d_queries[rows], early(0, 1)) + nt(r.d_keyval[rows], early(1, 2))
+        r.scores[:nodes, :width] = nt(r.d_queries[rows], early(0, 1)) + nt(r.d_keyval[rows], early(1, 2))
         return copies
 
     def norm_gradient(s, units, inverses, which):
@@ -595,7 +579,7 @@
         def norm(b):
             part = block(b, 64)
             unit = units[s, part].astype(WIDE)
-            d_out = r.d_normed[part]
+            d_out = r.scores[part, :width]
             d_scale = jnp.sum(d_out * unit, axis=0, keepdims=True)
             d_shift = jnp.sum(d_out, axis=0, keepdims=True)
             r.d_wave[s, which : which + 1] += d_scale
@@ -611,9 +595,46 @@
         rows = slice(s * nodes, (s + 1) * nodes)
         for copy in copies:
             copy.wait()
-        r.d_normed[...] += tn(r.send_hot[...], r.returned[s])
+        r.scores[:nodes, :width] += tn(r.send_hot[...], r.returned[s])
         norm_gradient(s, r.unit_one, r.inv_one, 0)
         r.d_summed[rows] = (r.start[...] * r.inv_count[...]).astype(LOW)
+
+    if not gathered:
+        late = Fold((r.g_up, r.g_down), (r.w_up, r.w_down), outs[1:3], r.fold, 1, where)
+        soon_fold = Fold((r.g_early,), (r.w_early,), outs[:1], r.fold, 0, where)
+    fold_steps = []
+
+    def announce(which):
+        if not gathered:
+            for other in folders:
+                pl.semaphore_signal(r.ready.at[which], inc=1, device_id=other, device_id_type=MESH)
+
+    def products_late():
+        planes = range(4) if gathered else far_planes(z)
+        for k, p in enumerate(planes):
+            r.g_down[p] = tn(r.gated[:, block(p, hidden // 4)], r.d_branch[...]).astype(LOW).reshape(r.g_down.shape[1:])
+            r.g_up[p] = tn(r.second[:, block(p, width // 4)], r.slope[...]).astype(LOW).reshape(r.g_up.shape[1:])
+            if gathered:
+                continue
+            if k == 0:
+                pl.semaphore_wait(r.ready.at[0], len(folders))
+            late.start(k)
+            if k > 0:
+                late.chip(k - 1)
+            if k > 1:
+                late.turn(k - 2)
+            if k > 2:
+                late.leave(k - 3)
+        if not gathered:
+            do = functools.partial
+            fold_steps.extend([
+                do(late.chip, 3), do(late.turn, 2), do(late.leave, 1), do(late.turn, 3), do(late.leave, 2),
+                do(late.leave, 3)])
+
+    def put_early(i, first, value):
+        value = value.astype(LOW)
+        r.g_early[2 * i : 2 * i + 2, :, :, :, :, first : first + value.shape[1]] = value.reshape(
+            (2, 2, 2, 2, width // 32, value.shape[1]))
 
     copies = encode(0)
     nodes_out = attend(0, copies)
@@ -624,17 +645,19 @@
         r.state[:, cols] = c_skip[0] * r.state[:, cols] + c_out[0] * out + level[1] * r.extra[:, cols]
 
     loop(tiles, decode_one)
+    load_target = load(target, r.extra, 3)
     copies = encode(1)
     nodes_out_two = attend(1, copies)
-    loss[...] = jnp.zeros(loss.shape, WIDE)
+    r.lost[...] = jnp.zeros(r.lost.shape, WIDE)
+    load_target.wait()
 
     def decode_two(t):
         cols = block(t, tile)
         out = nn(nodes_out_two, r.node_hot[:, cols])
         place = lax.broadcasted_iota(jnp.int32, (1, tile), 1) + t * tile
-        error = c_skip[1] * r.state[:, cols] + c_out[1] * out - r.aim[:, cols]
+        error = c_skip[1] * r.state[:, cols] + c_out[1] * out - r.extra[:, cols]
         error = jnp.where(place < counts[1], error, 0.0)
-        loss[...] += jnp.sum(error * error)
+        r.lost[...] += jnp.sum(error * error)
         r.extra[:, cols] = 2.0 * error
         r.low_state[:rows_used, cols] = (c_out[1] * 2.0 * error).astype(LOW)
 
@@ -651,38 +674,19 @@
 
     loop(tiles, into_one)
     copies = gradient(0)
-
-    stores = [None, None]
-
-    def store(slot, dst, cols):
-        copy = pltpu.make_async_copy(r.staged.at[slot, :, :cols], dst, r.stores.at[slot])
-        copy.start()
-        stores[slot] = copy
-
-    done = [0]
-
-    def product(left, i, right, out, first):
-        slot, cols = done[0] % 2, right.shape[1]
-        done[0] += 1
-        if stores[slot] is not None:
-            stores[slot].wait()
-        r.staged[slot, :, :cols] = tn(left[:, i * 256 : (i + 1) * 256], right[...]).astype(LOW)
-        store(slot, out.at[i * 256 : (i + 1) * 256, first : first + cols], cols)
-
-    for i in range(hidden // 256):
-        product(r.gated, i, r.d_branch, g_down, 0)
-    for i in range(width // 256):
-        product(r.second, i, r.slope, g_wide, at[2])
-        product(r.mixed, i, r.d_attn, g_wide, at[1])
-        product(r.final, i, r.taken, g_wide, at[4])
-        product(r.normed, i, r.d_keyval, g_wide, width)
-        product(r.normed.at[: 2 * nodes], i, r.d_queries, g_wide, 0)
+    announce(1)
+    for i in range(2):
+        cols = slice(i * width // 2, (i + 1) * width // 2)
+        put_early(i, 0, tn(r.normed[: 2 * nodes, cols], r.d_queries[...]))
+        advance(fold_steps, 1)
+        put_early(i, width, tn(r.normed[:, cols], r.d_keyval[...]))
+        put_early(i, w_at[2], tn(r.mixed[:, cols], r.d_attn[...]))
+        put_early(i, w_at[5], tn(r.final[:, cols], r.taken[...]))
+        advance(fold_steps, 1)
     absorb(0, copies)
-    for i in range(width // 256):
-        product(r.d_summed, i, r.sums, g_wide, at[3])
+    advance(fold_steps, len(fold_steps))
     for i in range(2):
-        slot = (done[0] + i) % 2
-        stores[slot].wait()
+        put_early(i, w_at[3], tn(r.d_summed[:, i * width // 2 : (i + 1) * width // 2], r.sums[...]))
         total = jnp.zeros((16, 16, 128), WIDE)
         for s in range(2):
             pieces = []
@@ -691,12 +695,45 @@
                 turned = pltpu.roll(piece, 64, 1)
                 pieces.append(jnp.where(lane < 64, piece, turned))
                 pieces.append(jnp.where(lane < 64, turned, piece))
-            rows = jnp.concatenate(pieces, axis=0)
-            total = total + rows[:, None, :] * waves[s][None]
-        r.staged[slot, :, :128] = total.reshape(256, 128).astype(LOW)
-        store(slot, g_wide.at[i * 256 : (i + 1) * 256, at[5] : at[5] + 128], 128)
-    for copy in stores:
-        copy.wait()
+            total = total + jnp.concatenate(pieces, axis=0)[:, None, :] * waves[s][None]
+        put_early(i, w_at[6], total.reshape(256, 128))
+    if gathered:
+        for i, src in enumerate((r.g_early, r.g_up, r.g_down)):
+            load(src, outs[i], 4 + i).wait()
+        outs[3][...] = r.lost[...]
+        return
+
+    pl.semaphore_wait(r.ready.at[1], len(folders))
+    for k in range(4):
+        soon_fold.start(k)
+    for k in range(4):
+        soon_fold.chip(k)
+    late.end()
+    squares = jnp.sum(outs[1][...] * outs[1][...]) + jnp.sum(outs[2][...] * outs[2][...])
+    for k in range(4):
+        soon_fold.turn(k)
+    for k in range(4):
+        soon_fold.leave(k)
+    soon_fold.end()
+    squares = squares + jnp.sum(outs[0][...] * outs[0][...])
+    row = lax.broadcasted_iota(jnp.int32, (8, 128), 0)
+    live = (chan * jnp.minimum(counts[1], pixels)).astype(WIDE)
+    mine = y * 4 + x * 2 + c
+    r.board[mine] = jnp.where(row == 0, squares, jnp.where(row == 1, r.lost[...], live))
+    more = []
+    for m, device in enumerate(plane_peers):
+        more.append(send(r.board.at[mine], r.board.at[mine], r.small, (m,), device))
+    for copy in more:
+        copy.wait_recv()
+    r.board[8 + z] = sum(r.board[m] for m in range(1, 8)) + r.board[0]
+    level_copies = [send(r.board.at[8 + z], r.board.at[8 + z], r.small, (7 + d,), along_z[d]) for d in (1, 2, 3)]
+    for copy in level_copies:
+        copy.wait_recv()
+    outs[3][...] = r.board[8] + r.board[9] + r.board[10] + r.board[11]
+    late.drain()
+    soon_fold.drain()
+    for copy in more + level_copies:
+        copy.wait_send()
 
 
 def run_net(chan, gathered, numbers, counts, previous, noisy, target, noise, owners, decode_idx, near_idx, send_idx,
@@ -705,13 +742,15 @@
     scratch = net_scratch(nodes, send_idx.shape[0] // 2, pixels, width, hidden, noisy.shape[0])
     vmem, smem = pl.BlockSpec(memory_space=pltpu.VMEM), pl.BlockSpec(memory_space=pltpu.SMEM)
     hbm = pl.BlockSpec(memory_space=pl.ANY)
-    wide = 4 * width + hidden + 4 * HALF_COLS
+    if gathered:
+        results = [(GRID + (width // 32, 5 * width), LOW), (GRID + (width // 32, hidden), LOW), (GRID + (hidden // 32, width), LOW)]
+    else:
+        results = [((width // 32, 5 * width), WIDE), ((width // 32, hidden), WIDE), ((hidden // 32, width), WIDE)]
     return pl.pallas_call(
         functools.partial(net_kernel, tuple(scratch), chan, gathered),
-        out_shape=[jax.ShapeDtypeStruct((width, wide), LOW), jax.ShapeDtypeStruct((hidden, width), LOW),
-                   jax.ShapeDtypeStruct((8, 128), WIDE)],
+        out_shape=[jax.ShapeDtypeStruct(shape, kind) for shape, kind in results + [((8, 128), WIDE)]],
         in_specs=[smem] * 2 + [hbm] * 4 + [vmem] * 5 + [hbm if gathered else vmem] * len(weights),
-        out_specs=[hbm, hbm, vmem],
+        out_specs=[hbm if gathered else vmem] * 3 + [vmem],
         scratch_shapes=list(scratch.values()),
         compiler_params=pltpu.CompilerParams(
             collective_id=3, has_side_effects=True, vmem_limit_bytes=VMEM_LIMIT),
@@ -745,7 +784,7 @@
         all_up = lax.all_gather(w_up.astype(LOW), BOTH, axis=0, tiled=True)
         all_down = lax.all_gather(w_down.astype(LOW), BOTH, axis=0, tiled=True)
         weights = [w.reshape(GRID + (-1, w.shape[1])) for w in (early, all_up, all_down)]
-    at = [0, 3 * width, 4 * width, 4 * width + hidden, 4 * width + hidden + 256, 4 * width + hidden + 384]
+    at = [0, 3 * width, 4 * width] + [4 * width + HALF_COLS * i for i in range(1, 4)]
 
     levels = noise_level[0]
     pixels = pixel_owner.shape[1]
@@ -760,33 +799,31 @@
     counts = jnp.concatenate([node_count[0], pixel_count[0]])
     waves = jnp.stack([fourier(levels[i]).reshape(FOUR // 2, 2) for i in range(2)])
     waves = jnp.repeat(waves, 64, axis=2)
-    g_wide, g_down, loss_local = run_net(
+    s_early, s_up, s_down, totals = run_net(
         channels, not small_slice, numbers, counts, previous, noisy, target, noise_two, pixel_owner, mesh_to_grid[0],
         neighbours[0].T, halo_send.reshape(-1, 1), waves, width, hidden, weights,
     )
-    count_local = (channels * jnp.minimum(pixel_count[0, 0], pixels)).astype(WIDE)
     if small_slice:
-        row = lax.broadcasted_iota(jnp.int32, (8, 128), 0)
-        extra = jnp.where(row == 1, loss_local, 0.0) + jnp.where(row == 2, count_local, 0.0)
-        s_wide, s_down, totals = reduce_scatter(g_wide, g_down, extra)
         totals = totals[:3, 0]
-        s_noise = s_wide[:, at[5] :].reshape(FOUR, -1)
+        s_noise = s_early[:, at[5] :].reshape(FOUR, -1)
     else:
-        g_noise = g_wide[:, at[5] :].reshape(-1, FOUR, 64).transpose(1, 0, 2).reshape(FOUR, -1)
-        s_wide = lax.psum_scatter(g_wide[:, : at[5]].astype(WIDE), BOTH, scatter_dimension=0, tiled=True)
-        s_down = lax.psum_scatter(g_down.astype(WIDE), BOTH, scatter_dimension=0, tiled=True)
+        g_early = s_early.reshape(width, -1)
+        g_noise = g_early[:, at[5] :].reshape(-1, FOUR, 64).transpose(1, 0, 2).reshape(FOUR, -1)
+        parts = (g_early[:, : at[5]], s_up.reshape(width, -1), s_down.reshape(hidden, -1))
+        s_early, s_up, s_down = (
+            lax.psum_scatter(g.astype(WIDE), BOTH, scatter_dimension=0, tiled=True) for g in parts)
         s_noise = lax.psum_scatter(g_noise.astype(WIDE), BOTH, scatter_dimension=1, tiled=True)
-        squares = jnp.sum(s_wide * s_wide) + jnp.sum(s_down * s_down) + jnp.sum(s_noise * s_noise)
-        totals = lax.psum((squares, loss_local[0, 0], count_local), BOTH)
-    second = at[3] + HALF_COLS
+        squares = sum(jnp.sum(shard * shard) for shard in (s_early, s_up, s_down, s_noise))
+        count_local = (channels * jnp.minimum(pixel_count[0, 0], pixels)).astype(WIDE)
+        totals = lax.psum((squares, totals[0, 0], count_local), BOTH)
     shards = (
-        jnp.concatenate([s_wide[:, at[3] : at[3] + channels], s_wide[:, second : second + channels]], axis=1).T,
-        s_wide[:, : at[1]],
-        s_wide[:, at[1] : at[2]],
-        s_wide[:, at[2] : at[3]],
+        jnp.concatenate([s_early[:, at[2] : at[2] + channels], s_early[:, at[3] : at[3] + channels]], axis=1).T,
+        s_early[:, : at[1]],
+        s_early[:, at[1] : at[2]],
+        s_up,
         s_down,
         s_noise,
-        s_wide[:, at[4] : at[4] + channels],
+        s_early[:, at[4] : at[4] + channels],
     )
     grad_norm = jnp.sqrt(totals[0])
     factor = THRESHOLD / jnp.maximum(grad_norm, THRESHOLD)

time: 227 us -> 207 us (0.912)
  Pallas kernels: 191 us -> 168 us
  other arithmetic: 9.85 us -> 14 us
    pallas_call x1 -> x0, Pallas kernels: 56.7 us -> none  [reduce_scatter(): pl.pallas_call(scatter_kernel, out_shape=[jax.ShapeDtypeStruct((r, n), WI...]
    pallas_call x1, Pallas kernels: 135 us -> 168 us  [run_net(): pl.pallas_call(functools.partial(net_kernel, tuple(scratch), chan, gather...]
    sub x7, other arithmetic: 4.99 us -> 9.17 us  [on_device(): new_weights.append(w - LEARN_RATE * (stepped + DECAY_RATE * w))]
where the time goes in v1:
time: 207 us; the launch traced here: 203 us
  Pallas kernels  168 us (81%)
  local copies, waits for them, and re-layouts  15.6 us (8%)
  other arithmetic  14 us (7%)
  between operations  5.58 us (3%)
    pallas_call x1, Pallas kernels, run_net(): pl.pallas_call(functools.partial(net_kernel, tuple(scratch), chan, gather...  168 us
    sub x7, other arithmetic, on_device(): new_weights.append(w - LEARN_RATE * (stepped + DECAY_RATE * w))  9.17 us

profile of v1, /device:TPU:0, one launch (start us, length us, event | category | flops | bytes accessed | tf_op | source)
XLA Modules:
  0.0 202.9 jit_solution(1224070376385121028)
XLA Ops:
  0.7 1.3 fusion.29
  2.7 0.1 pad_maximum_fusion.2
  2.8 0.1 stack_reshape.6
  3.6 0.1 pad_maximum_fusion.3
  3.7 0.1 stack_reshape.7
  3.8 0.1 broadcast_in_dim.4
  3.9 0.7 reshape.117.waves
  4.6 0.7 fusion.18
  5.3 0.7 pad_maximum_fusion.1
  5.9 0.1 copy.73
  6.0 0.6 reshape.115.numbers
  6.6 4.1 %fusion.26 = (f32[1,1,84,3072]{3,1,2,0:T(1,128)S(1)}, f32[1,1,84,3072]{3,1,2,0:T(1,128)S(1)}) fusion(f32[1,2,84,3072]{3,1,2,0:T(2,128)} %param.33), kind=kLoop, calls=%fused_computation.60 | loop fusion | bytes 4128768 | tf_op jit(solution)/shard_map/slice | solution.py:796
  10.7 0.0 copy-done
  10.7 1.0 fusion.2
  11.7 1.2 pad.17.noisy
  12.8 0.2 copy.95
  13.0 0.0 copy-start.10
  13.0 1.1 pad.19.noise
  14.2 0.7 fusion.27
  14.8 0.2 copy.96
  15.0 0.0 copy-start.1
  15.0 1.1 pad.18.target
  16.2 0.5 copy-done.1
  16.7 0.2 copy.97
  16.8 0.0 copy-start.12
  16.8 0.0 copy-start.11
  16.9 1.0 fusion.previous
  17.8 0.7 copy.77.send_idx
  18.6 0.0 copy-done.12
  18.6 0.6 copy.98
  19.2 0.7 reshape.118.rest_5_
  21.2 0.6 pad_add_fusion.counts
  21.8 167.8 %shard_map.478 = (f32[16,2560]{1,0:T(8,128)}, f32[16,2048]{1,0:T(8,128)}, f32[64,512]{1,0:T(8,128)}, f32[8,128]{1,0:T(8,128)}) custom-call(f32[8]{0:T(128)} %reshape.115.numbers, s32[2]{0:T(128)} %pad_add_fusion.counts, bf16[128,3072]{1,0:T(8,128)(2,1)} %fusion.previous, f32[96,3072]{1,0:T(8,128)} %pad.17.noisy, f32[96,3072]{1,0:T(8,128)} %pad.18.target, ...), custom_call_target="tpu_custom_call" | custom-call | tf_op jit(solution)/shard_map/pallas_call | solution.py:749
  189.5 0.0 copy-start.2
  189.5 0.0 copy-start.4
  189.5 0.0 copy-start.5
  189.6 1.3 fusion.28
  191.6 1.4 multiply_subtract_fusion.6
  193.0 0.0 copy-start.8
  193.0 1.5 multiply_subtract_fusion.5
  194.6 0.7 slice_multiply_fusion.3
  195.3 0.1 mul.419
  195.3 1.4 multiply_subtract_fusion.4
  196.7 1.5 multiply_subtract_fusion.3
  198.2 1.8 multiply_subtract_fusion.2
  200.0 0.0 copy-done.4
  200.0 0.8 multiply_subtract_fusion
  200.8 0.8 multiply_subtract_fusion.1
  (19 shorter events, 0.1 us)
Async XLA Ops:
  6.6 4.1 %copy-start = (f32[1,84,3072]{2,0,1:T(1,128)S(1)}, f32[1,84,3072]{2,0,1:T(1,128)}, u32[]{:S(2)}) copy-start(f32[1,84,3072]{2,0,1:T(1,128)} %param.32) | copy-start | bytes 3096580
  13.0 1.1 copy-start.10
  15.0 1.6 copy-start.1
  16.7 1.2 copy-start.13
  16.8 1.7 copy-start.12
  16.8 2.4 %copy-start.11 = (f32[32,64]{1,0:T(8,128)S(1)}, f32[32,64]{1,0:T(8,128)}, u32[]{:S(2)}) copy-start(f32[32,64]{1,0:T(8,128)} %param.46) | copy-start | bytes 24580
  189.5 10.4 %copy-start.2 = (f32[64,512]{1,0:T(8,128)S(1)}, f32[64,512]{1,0:T(8,128)}, u32[]{:S(2)}) copy-start(f32[64,512]{1,0:T(8,128)} %rest_7_.1) | copy-start | bytes 393220
  189.5 10.4 %copy-start.4 = (f32[64,512]{1,0:T(8,128)S(1)}, f32[64,512]{1,0:T(8,128)}, u32[]{:S(2)}) copy-start(f32[64,512]{1,0:T(8,128)} %param.52) | copy-start | bytes 393220
  189.5 10.4 %copy-start.5 = (f32[64,512]{1,0:T(8,128)S(1)}, f32[64,512]{1,0:T(8,128)}, u32[]{:S(2)}) copy-start(f32[64,512]{1,0:T(8,128)} %param.59) | copy-start | bytes 393220
  189.6 10.4 %copy-start.9 = (f32[64,512]{1,0:T(8,128)S(1)}, f32[64,512]{1,0:T(8,128)}, u32[]{:S(2)}) copy-start(f32[64,512]{1,0:T(8,128)} %get-tuple-element.31) | copy-start | bytes 393220
  193.0 7.8 %copy-start.3 = (f32[16,2048]{1,0:T(8,128)S(1)}, f32[16,2048]{1,0:T(8,128)}, u32[]{:S(2)}) copy-start(f32[16,2048]{1,0:T(8,128)} %rest_6_.1) | copy-start | bytes 393220
  193.0 7.8 %copy-start.6 = (f32[16,2048]{1,0:T(8,128)S(1)}, f32[16,2048]{1,0:T(8,128)}, u32[]{:S(2)}) copy-start(f32[16,2048]{1,0:T(8,128)} %param.51) | copy-start | bytes 393220
  193.0 7.8 %copy-start.7 = (f32[16,2048]{1,0:T(8,128)S(1)}, f32[16,2048]{1,0:T(8,128)}, u32[]{:S(2)}) copy-start(f32[16,2048]{1,0:T(8,128)} %param.58) | copy-start | bytes 393220
  193.0 7.8 %copy-start.8 = (f32[16,2048]{1,0:T(8,128)S(1)}, f32[16,2048]{1,0:T(8,128)}, u32[]{:S(2)}) copy-start(f32[16,2048]{1,0:T(8,128)} %get-tuple-element.30) | copy-start | bytes 393220

commit v2 on v1

--- a/solution.py
+++ b/solution.py
@@ -39,12 +39,6 @@
 
 def tn(a, b):
     return lax.dot_general(a, b, (((0,), (0,)), ((), ())), preferred_element_type=WIDE)
-
-
-def fourier(level):
-    frequency = 0.25 * (jnp.arange(FOUR // 2).astype(jnp.float32) + 1.0)
-    angles = jnp.log(level) * frequency
-    return jnp.concatenate([jnp.sin(angles), jnp.cos(angles)])
 
 
 def norm_parts(hidden):
@@ -93,7 +87,7 @@
         owner_hot=pltpu.VMEM((nodes, pixels), LOW),
         node_hot=pltpu.VMEM((nodes, pixels), LOW),
         bias=pltpu.VMEM((near, nodes), WIDE),
-        send_hot=pltpu.VMEM((2 * halo, nodes), LOW),
+        send_hot=pltpu.VMEM((nodes, 2 * halo), LOW),
         inv_count=pltpu.VMEM((nodes, 1), WIDE),
         sums=pltpu.VMEM((2 * nodes, 2 * HALF_COLS), LOW),
         wave=pltpu.VMEM((2, 4, width), WIDE),
@@ -125,11 +119,13 @@
         returned=pltpu.VMEM((2, 2 * halo, width), LOW),
         state=pltpu.VMEM((kept, pixels), WIDE),
         extra=pltpu.VMEM((kept, pixels), WIDE),
-        low_state=pltpu.VMEM((HALF_COLS, pixels), LOW),
+        low_state=pltpu.VMEM((kept, pixels), LOW),
         g_early=pltpu.VMEM(GRID + (width // 32, 5 * width), LOW),
         g_up=pltpu.VMEM(GRID + (width // 32, hidden), LOW),
         g_down=pltpu.VMEM(GRID + (hidden // 32, width), LOW),
         lost=pltpu.VMEM((8, 128), WIDE),
+        noise_rows=pltpu.VMEM((FOUR // 2, 128), WIDE),
+        waves=pltpu.VMEM((2, FOUR // 2, 128), WIDE),
         board=pltpu.VMEM((12, 8, 128), WIDE),
         w_early=pltpu.VMEM(GRID + (width // 32, 5 * width), LOW),
         w_up=pltpu.VMEM(GRID + (width // 32, hidden), LOW),
@@ -289,13 +285,14 @@
             copy.wait_send()
 
 
-def net_kernel(names, chan, gathered, numbers, counts, previous, noisy, target, noise, owners, decode_idx, near_idx,
-               send_idx, waves, *rest):
+def net_kernel(names, gathered, levels, node_count, pixel_count, previous, noisy, target, noise, owners, decode_idx,
+               near_idx, send_idx, *rest):
     outs = rest[-4 - len(names) : -len(names)]
     weights, scratch = rest[: -4 - len(names)], rest[-len(names) :]
     r = types.SimpleNamespace(**dict(zip(names, scratch)))
     nodes, pixels = near_idx.shape[1], owners.shape[1]
-    halo = send_idx.shape[0] // 2
+    waves = r.waves
+    halo, chan = send_idx.shape[1] // 2, previous.shape[0]
     near = nodes + 2 * halo
     width, hidden = r.start.shape[1], r.gated.shape[1]
     at = [0, 3 * width, 4 * width, 4 * width + hidden, 4 * width + hidden + 256, 4 * width + hidden + 384]
@@ -321,9 +318,7 @@
         copy.start()
         return copy
 
-    pairs = ((previous, r.low_state), (noisy, r.state), (noise, r.extra))
-    loads = [load(src, dst, slot) for slot, (src, dst) in enumerate(pairs)]
-    rows_used = r.state.shape[0]
+    loads = [load(previous, r.extra, 0), load(noisy, r.state, 1)]
     w_at = [0, width, 3 * width, 4 * width, 4 * width + HALF_COLS, 4 * width + 2 * HALF_COLS, 4 * width + 3 * HALF_COLS]
     w_targets = (r.w_early, r.w_up, r.w_down)
     early_steps, late_steps = [], []
@@ -333,6 +328,10 @@
             load(src, dst, 4 + i).wait()
     else:
         project, output, encode_prev, encode_noisy, decode, noise_rows, up, down = weights
+        for i in range(FOUR // 2):
+            r.noise_rows[i : i + 1, :64] = noise_rows[2 * i : 2 * i + 1]
+            r.noise_rows[i : i + 1, 64:] = noise_rows[2 * i + 1 : 2 * i + 2]
+        noise_rows = r.noise_rows
         r.w_early[z, y, x, c, :, 4 * width :] = jnp.zeros((width // 32, width), LOW)
         for i, piece in ((0, project), (2, output), (3, encode_prev), (4, encode_noisy), (5, decode), (6, noise_rows)):
             r.w_early[z, y, x, c, :, w_at[i] : w_at[i] + piece.shape[1]] = piece[...].astype(LOW)
@@ -342,6 +341,11 @@
         late_steps = spread_steps(w_targets[1:], r.spread, 1, where)
         pl.semaphore_wait(barrier, len(others))
 
+    def encode_state(s):
+        r.low_state[...] = (r.state[...] * c_in[s]).astype(LOW)
+        r.sums[s * nodes : (s + 1) * nodes, HALF_COLS : HALF_COLS + chan] = nt(
+            r.owner_hot[...], r.low_state[...]).astype(LOW)
+
     def advance(steps, count):
         for _ in range(min(count, len(steps))):
             steps.pop(0)()
@@ -354,15 +358,24 @@
 
     advance(early_steps, 1)
 
-    level = [numbers[4 * s] for s in range(2)]
-    c_in = [numbers[4 * s + 1] for s in range(2)]
-    c_skip = [numbers[4 * s + 2] for s in range(2)]
-    c_out = [numbers[4 * s + 3] for s in range(2)]
+    level = [levels[0, s] for s in range(2)]
+    c_in, c_skip, c_out = [], [], []
+    for s in range(2):
+        whole = jnp.full((8, 128), level[s], WIDE)
+        scaled = lax.rsqrt(whole * whole + 1.0)
+        c_in.append(scaled[:1, :1])
+        c_skip.append((1.0 / (whole * whole + 1.0))[:1, :1])
+        c_out.append((whole * scaled)[:1, :1])
+        shape = (FOUR // 2, 128)
+        feature = 2 * lax.broadcasted_iota(jnp.int32, shape, 0) + lax.broadcasted_iota(jnp.int32, shape, 1) // 64
+        frequency = 0.25 * ((feature % (FOUR // 2)).astype(WIDE) + 1.0)
+        angle = jnp.log(jnp.full(shape, level[s], WIDE)) * frequency
+        waves[s] = jnp.where(feature < FOUR // 2, jnp.sin(angle), jnp.cos(angle))
 
     def build_hot(t):
         cols = block(t, tile)
         place = lax.broadcasted_iota(jnp.int32, (1, tile), 1) + t * tile
-        own = jnp.where(place < counts[1], owners[:, cols], -1)
+        own = jnp.where(place < pixel_count[0], owners[:, cols], -1)
         three = [decode_idx[i : i + 1, cols] for i in range(3)]
 
         def rows(b):
@@ -380,7 +393,7 @@
         listed = jnp.zeros((32, nodes), WIDE)
         for j in range(1, NEIGH):
             listed = listed + (near_idx[j : j + 1] == place).astype(WIDE)
-        listed = jnp.where((place >= nodes) | (place < counts[0]), listed, 0.0)
+        listed = jnp.where((place >= nodes) | (place < node_count[0]), listed, 0.0)
         listed = listed + (near_idx[0:1] == place).astype(WIDE)
         r.bias[rows] = jnp.where(listed > 0.0, jnp.log(jnp.maximum(listed, 1.0)), -1e30)
 
@@ -391,21 +404,21 @@
         build_hot(t)
         advance(early_steps, 2)
     r.send_hot[...] = (
-        lax.broadcasted_iota(jnp.int32, (2 * halo, nodes), 1) == send_idx[...]
+        lax.broadcasted_iota(jnp.int32, (nodes, 2 * halo), 0) == send_idx[...]
     ).astype(WIDE).astype(LOW)
 
     loads[0].wait()
-    summed = nt(r.owner_hot[...], r.low_state[...])
-    channel = lax.broadcasted_iota(jnp.int32, (nodes, HALF_COLS), 1)
-    total = jnp.sum(jnp.where(channel == chan, summed, 0.0), axis=1, keepdims=True)
+    total = nt(r.owner_hot[...], jnp.ones((8, pixels), LOW))[:, :1]
     r.inv_count[...] = 1.0 / jnp.maximum(total, 1.0)
-    summed = jnp.where(channel < chan, summed, 0.0).astype(LOW)
-    r.sums[:nodes, :HALF_COLS] = summed
-    r.sums[nodes:, :HALF_COLS] = summed
-    for copy in loads[1:]:
-        copy.wait()
-    r.low_state[:rows_used] = (r.state[...] * c_in[0]).astype(LOW)
-    r.sums[:nodes, HALF_COLS:] = nt(r.owner_hot[...], r.low_state[...]).astype(LOW)
+    r.sums[...] = jnp.zeros(r.sums.shape, LOW)
+    r.taken[...] = jnp.zeros(r.taken.shape, LOW)
+    r.low_state[...] = r.extra[...].astype(LOW)
+    load_noise = load(noise, r.extra, 2)
+    summed = nt(r.owner_hot[...], r.low_state[...]).astype(LOW)
+    r.sums[:nodes, :chan] = summed
+    r.sums[nodes:, :chan] = summed
+    loads[1].wait()
+    encode_state(0)
     advance(early_steps, len(early_steps))
     advance(late_steps, 3)
 
@@ -434,8 +447,7 @@
     def encode(s):
         rows = slice(s * nodes, (s + 1) * nodes)
         if s:
-            r.low_state[:rows_used] = (r.state[...] * c_in[s]).astype(LOW)
-            r.sums[rows, HALF_COLS:] = nt(r.owner_hot[...], r.low_state[...]).astype(LOW)
+            encode_state(s)
         r.start[...] = nt(r.sums[rows], early(3, 5)) * r.inv_count[...]
 
         def norm(b):
@@ -448,7 +460,7 @@
 
         loop(nodes // 64, norm)
         normed = r.normed[rows]
-        r.outgoing[s] = nn(r.send_hot[...], normed).astype(LOW)
+        r.outgoing[s] = tn(r.send_hot[...], normed).astype(LOW)
         first = 2 * nodes + 2 * halo * s
         copies = pass_on(s, r.normed.at[first + halo : first + 2 * halo], r.normed.at[first : first + halo])
         r.queries[s] = nn(normed, early(0, 1)).astype(LOW)
@@ -514,13 +526,12 @@
         loop(hidden // 256, feed)
         r.final[rows] = (r.start[...] + nn(r.gated[rows], r.w_down[...].reshape(hidden, width))).astype(LOW)
         out = nn(r.final[rows], early(5, 6)) * (1.0 / 3.0)
-        return out.T.astype(LOW)[:rows_used]
+        return out.T[:chan].astype(LOW)
 
     def gradient(s):
         rows = slice(s * nodes, (s + 1) * nodes)
-        taken = (nt(r.node_hot[...], r.low_state[...]) * (1.0 / 3.0)).astype(LOW)
-        r.taken[rows] = taken
-        d_final = nt(taken, early(5, 6))
+        r.taken[rows, :chan] = (nt(r.node_hot[...], r.low_state[...]) * (1.0 / 3.0)).astype(LOW)
+        d_final = nt(r.taken[rows], early(5, 6))
         r.start[...] = d_final
         r.d_branch[rows] = d_final.astype(LOW)
 
@@ -595,7 +606,7 @@
         rows = slice(s * nodes, (s + 1) * nodes)
         for copy in copies:
             copy.wait()
-        r.scores[:nodes, :width] += tn(r.send_hot[...], r.returned[s])
+        r.scores[:nodes, :width] += nn(r.send_hot[...], r.returned[s])
         norm_gradient(s, r.unit_one, r.inv_one, 0)
         r.d_summed[rows] = (r.start[...] * r.inv_count[...]).astype(LOW)
 
@@ -639,6 +650,8 @@
     copies = encode(0)
     nodes_out = attend(0, copies)
 
+    load_noise.wait()
+
     def decode_one(t):
         cols = block(t, tile)
         out = nn(nodes_out, r.node_hot[:, cols])
@@ -656,21 +669,21 @@
         out = nn(nodes_out_two, r.node_hot[:, cols])
         place = lax.broadcasted_iota(jnp.int32, (1, tile), 1) + t * tile
         error = c_skip[1] * r.state[:, cols] + c_out[1] * out - r.extra[:, cols]
-        error = jnp.where(place < counts[1], error, 0.0)
+        error = jnp.where(place < pixel_count[0], error, 0.0)
         r.lost[...] += jnp.sum(error * error)
         r.extra[:, cols] = 2.0 * error
-        r.low_state[:rows_used, cols] = (c_out[1] * 2.0 * error).astype(LOW)
+        r.low_state[:, cols] = (c_out[1] * 2.0 * error).astype(LOW)
 
     loop(tiles, decode_two)
     copies = gradient(1)
     absorb(1, copies)
     d_nodes = nn(r.d_summed[nodes:], early(4, 5))
-    d_nodes = d_nodes.T.astype(LOW)[:rows_used]
+    d_nodes = d_nodes.T[:chan].astype(LOW)
 
     def into_one(t):
         cols = block(t, tile)
         d_noisy = c_skip[1] * r.extra[:, cols] + c_in[1] * nn(d_nodes, r.owner_hot[:, cols])
-        r.low_state[:rows_used, cols] = (c_out[0] * d_noisy).astype(LOW)
+        r.low_state[:, cols] = (c_out[0] * d_noisy).astype(LOW)
 
     loop(tiles, into_one)
     copies = gradient(0)
@@ -717,7 +730,7 @@
     soon_fold.end()
     squares = squares + jnp.sum(outs[0][...] * outs[0][...])
     row = lax.broadcasted_iota(jnp.int32, (8, 128), 0)
-    live = (chan * jnp.minimum(counts[1], pixels)).astype(WIDE)
+    live = (chan * jnp.minimum(pixel_count[0], pixels)).astype(WIDE)
     mine = y * 4 + x * 2 + c
     r.board[mine] = jnp.where(row == 0, squares, jnp.where(row == 1, r.lost[...], live))
     more = []
@@ -736,10 +749,10 @@
         copy.wait_send()
 
 
-def run_net(chan, gathered, numbers, counts, previous, noisy, target, noise, owners, decode_idx, near_idx, send_idx,
-            waves, width, hidden, weights):
+def run_net(gathered, levels, node_count, pixel_count, previous, noisy, target, noise, owners, decode_idx, near_idx, send_idx,
+            width, hidden, weights):
     nodes, pixels = near_idx.shape[1], owners.shape[1]
-    scratch = net_scratch(nodes, send_idx.shape[0] // 2, pixels, width, hidden, noisy.shape[0])
+    scratch = net_scratch(nodes, send_idx.shape[1] // 2, pixels, width, hidden, noisy.shape[0])
     vmem, smem = pl.BlockSpec(memory_space=pltpu.VMEM), pl.BlockSpec(memory_space=pltpu.SMEM)
     hbm = pl.BlockSpec(memory_space=pl.ANY)
     if gathered:
@@ -747,14 +760,64 @@
     else:
         results = [((width // 32, 5 * width), WIDE), ((width // 32, hidden), WIDE), ((hidden // 32, width), WIDE)]
     return pl.pallas_call(
-        functools.partial(net_kernel, tuple(scratch), chan, gathered),
+        functools.partial(net_kernel, tuple(scratch), gathered),
         out_shape=[jax.ShapeDtypeStruct(shape, kind) for shape, kind in results + [((8, 128), WIDE)]],
-        in_specs=[smem] * 2 + [hbm] * 4 + [vmem] * 5 + [hbm if gathered else vmem] * len(weights),
+        in_specs=[smem] * 3 + [hbm] * 4 + [vmem] * 4 + [hbm if gathered else vmem] * len(weights),
         out_specs=[hbm if gathered else vmem] * 3 + [vmem],
         scratch_shapes=list(scratch.values()),
         compiler_params=pltpu.CompilerParams(
             collective_id=3, has_side_effects=True, vmem_limit_bytes=VMEM_LIMIT),
-    )(numbers, counts, previous, noisy, target, noise, owners, decode_idx, near_idx, send_idx, waves, *weights)
+    )(levels, node_count, pixel_count, previous, noisy, target, noise, owners, decode_idx, near_idx, send_idx, *weights)
+
+
+def adam_kernel(packed, totals, *refs):
+    g_early, g_up, g_down = refs[:3]
+    given, made, (loss, count, norm, turned) = refs[-46:-25], refs[-25:-4], refs[-4:]
+    loss[...] = totals[1:2, 0:1]
+    count[...] = totals[2:3, 0:1]
+    norm[...] = jnp.sqrt(totals[0:1, 0:1])
+    factor = THRESHOLD / jnp.maximum(jnp.sqrt(totals[0:1, 0:1]), THRESHOLD)
+    width = refs[-46 + 6].shape[1]
+    at = [0, 3 * width, 4 * width] + [4 * width + HALF_COLS * i for i in range(1, 4)]
+    chan = given[0].shape[1] // 2
+
+    def update(i, at_in, g):
+        w, m, v = (given[3 * i + j][at_in] for j in range(3))
+        clipped = g * factor
+        moment = BETA_ONE * m + (1.0 - BETA_ONE) * clipped
+        variance = BETA_TWO * v + (1.0 - BETA_TWO) * clipped * clipped
+        stepped = (
+            moment
+            / (1.0 - BETA_ONE**STEP)
+            / (jnp.sqrt(variance / (1.0 - BETA_TWO**STEP)) + EPSILON)
+        )
+        made[3 * i][at_in] = w - LEARN_RATE * (stepped + DECAY_RATE * w)
+        made[3 * i + 1][at_in] = moment
+        made[3 * i + 2][at_in] = variance
+
+    whole = (slice(None), slice(None))
+    both = jnp.concatenate([g_early[:, at[2] : at[2] + chan], g_early[:, at[3] : at[3] + chan]], axis=1)
+    update(0, whole, both)
+    update(1, whole, g_early[:, : at[1]])
+    update(2, whole, g_early[:, at[1] : at[2]])
+    update(3, whole, g_up[...])
+    update(4, whole, g_down[...])
+    for i in range(FOUR // 2 if packed else 0):
+        turned[2 * i : 2 * i + 1] = g_early[i : i + 1, at[5] : at[5] + 64]
+        turned[2 * i + 1 : 2 * i + 2] = g_early[i : i + 1, at[5] + 64 :]
+    update(5, whole, turned[...] if packed else refs[3][...])
+    update(6, whole, g_early[:, at[4] : at[4] + chan])
+
+
+def run_adam(totals, grads, given):
+    return pl.pallas_call(
+        functools.partial(adam_kernel, len(grads) == 3),
+        out_shape=[jax.ShapeDtypeStruct(shape, WIDE) for shape in [a.shape for a in given] + [(1, 1)] * 3],
+        in_specs=[pl.BlockSpec(memory_space=pltpu.VMEM)] * (1 + len(grads) + len(given)),
+        out_specs=[pl.BlockSpec(memory_space=pltpu.VMEM)] * (len(given) + 3),
+        scratch_shapes=[pltpu.VMEM((FOUR, 64), WIDE)],
+        compiler_params=pltpu.CompilerParams(vmem_limit_bytes=VMEM_LIMIT),
+    )(totals, *grads, *given)
 
 
 def fill(array, columns):
@@ -775,7 +838,7 @@
     flipped = w_encode.T
     halves = (flipped[:, :channels], flipped[:, channels:])
     if small_slice:
-        weights = (w_project, w_output) + halves + (w_decode, w_noise.reshape(rows, HALF_COLS), w_up, w_down)
+        weights = (w_project, w_output) + halves + (w_decode, w_noise, w_up, w_down)
     else:
         pieces = [w_project, w_output] + [fill(half, HALF_COLS) for half in halves] + [fill(w_decode, HALF_COLS)]
         early = lax.all_gather(jnp.concatenate(pieces, axis=1).astype(LOW), BOTH, axis=0, tiled=True)
@@ -786,27 +849,17 @@
         weights = [w.reshape(GRID + (-1, w.shape[1])) for w in (early, all_up, all_down)]
     at = [0, 3 * width, 4 * width] + [4 * width + HALF_COLS * i for i in range(1, 4)]
 
-    levels = noise_level[0]
     pixels = pixel_owner.shape[1]
-    padding = ((0, -channels % 16), (0, 0))
-    previous = jnp.concatenate([previous_state[0], jnp.ones((1, pixels), WIDE)], axis=0).astype(LOW)
-    previous = jnp.pad(previous, ((0, HALF_COLS - channels - 1), (0, 0)))
-    target = jnp.pad(target_state[0], padding)
-    noisy = jnp.pad(target_state[0] + levels[0] * noise_draws[0, 0], padding)
-    noise_two = jnp.pad(noise_draws[0, 1], padding)
-    c_in = lax.rsqrt(levels * levels + 1.0)
-    numbers = jnp.stack([levels, c_in, 1.0 / (levels * levels + 1.0), levels * c_in], axis=1).reshape(8)
-    counts = jnp.concatenate([node_count[0], pixel_count[0]])
-    waves = jnp.stack([fourier(levels[i]).reshape(FOUR // 2, 2) for i in range(2)])
-    waves = jnp.repeat(waves, 64, axis=2)
+    noisy = target_state[0] + noise_level[0, 0] * noise_draws[0, 0]
     s_early, s_up, s_down, totals = run_net(
-        channels, not small_slice, numbers, counts, previous, noisy, target, noise_two, pixel_owner, mesh_to_grid[0],
-        neighbours[0].T, halo_send.reshape(-1, 1), waves, width, hidden, weights,
+        not small_slice, noise_level, node_count[0], pixel_count[0], previous_state[0], noisy, target_state[0], noise_draws[0, 1],
+        pixel_owner, mesh_to_grid[0], neighbours[0].T, halo_send, width, hidden, weights,
     )
-    if small_slice:
-        totals = totals[:3, 0]
-        s_noise = s_early[:, at[5] :].reshape(FOUR, -1)
-    else:
+    masters = (w_encode, w_project, w_output, w_up, w_down, w_noise, w_decode)
+    moments = (m_encode, m_project, m_output, m_up, m_down, m_noise, m_decode)
+    seconds = (v_encode, v_project, v_output, v_up, v_down, v_noise, v_decode)
+    grads = (s_early, s_up, s_down)
+    if not small_slice:
         g_early = s_early.reshape(width, -1)
         g_noise = g_early[:, at[5] :].reshape(-1, FOUR, 64).transpose(1, 0, 2).reshape(FOUR, -1)
         parts = (g_early[:, : at[5]], s_up.reshape(width, -1), s_down.reshape(hidden, -1))
@@ -815,40 +868,14 @@
         s_noise = lax.psum_scatter(g_noise.astype(WIDE), BOTH, scatter_dimension=1, tiled=True)
         squares = sum(jnp.sum(shard * shard) for shard in (s_early, s_up, s_down, s_noise))
         count_local = (channels * jnp.minimum(pixel_count[0, 0], pixels)).astype(WIDE)
-        totals = lax.psum((squares, totals[0, 0], count_local), BOTH)
-    shards = (
-        jnp.concatenate([s_early[:, at[2] : at[2] + channels], s_early[:, at[3] : at[3] + channels]], axis=1).T,
-        s_early[:, : at[1]],
-        s_early[:, at[1] : at[2]],
-        s_up,
-        s_down,
-        s_noise,
-        s_early[:, at[4] : at[4] + channels],
-    )
-    grad_norm = jnp.sqrt(totals[0])
-    factor = THRESHOLD / jnp.maximum(grad_norm, THRESHOLD)
-    masters = (w_encode, w_project, w_output, w_up, w_down, w_noise, w_decode)
-    moments = (m_encode, m_project, m_output, m_up, m_down, m_noise, m_decode)
-    seconds = (v_encode, v_project, v_output, v_up, v_down, v_noise, v_decode)
-    new_weights, new_moments, new_seconds = ([], [], [])
-    for w, m, v, g in zip(masters, moments, seconds, shards):
-        clipped = g * factor
-        moment = BETA_ONE * m + (1.0 - BETA_ONE) * clipped
-        variance = BETA_TWO * v + (1.0 - BETA_TWO) * clipped * clipped
-        stepped = (
-            moment
-            / (1.0 - BETA_ONE**STEP)
-            / (jnp.sqrt(variance / (1.0 - BETA_TWO**STEP)) + EPSILON)
-        )
-        new_weights.append(w - LEARN_RATE * (stepped + DECAY_RATE * w))
-        new_moments.append(moment)
-        new_seconds.append(variance)
-    return (
-        tuple(new_weights)
-        + tuple(new_moments)
-        + tuple(new_seconds)
-        + (totals[1], totals[2], grad_norm)
-    )
+        sums = lax.psum((squares, totals[0, 0], count_local), BOTH)
+        totals = jnp.broadcast_to(jnp.stack(sums + sums[:1] * 5)[:, None], (8, 128))
+        grads = (s_early, s_up, s_down, s_noise)
+    given = [a for group in zip(masters, moments, seconds) for a in group]
+    given[:3] = [a.T for a in given[:3]]
+    *made, loss, count, norm = run_adam(totals, grads, given)
+    made[:3] = [a.T for a in made[:3]]
+    return tuple(made[0::3]) + tuple(made[1::3]) + tuple(made[2::3]) + tuple(a.reshape(()) for a in (loss, count, norm))
 
 
 def solution(mesh):

time: 207 us -> 187 us (0.903)
  other arithmetic: 14 us -> 1.35 us
  local copies, waits for them, and re-layouts: 15.6 us -> 9.96 us
  between operations: 5.58 us -> 2.19 us
  Pallas kernels: 168 us -> 171 us
    sub x7 -> x0, other arithmetic: 9.17 us -> none  [on_device(): new_weights.append(w - LEARN_RATE * (stepped + DECAY_RATE * w))]
    pad x3 -> x0, local copies, waits for them, and re-layouts: 3.4 us -> none  [the longest x1 1.16 us: on_device(): noisy = jnp.pad(target_state[0] + levels[0] * noise_draws[0, 0], padding)]
    pallas_call x1 -> x2, Pallas kernels: 168 us -> 171 us  [the longest x1 168 us: run_net(): pl.pallas_call(functools.partial(net_kernel, tuple(scratch), gathered), o...]
    unnamed x32 -> x9, local copies, waits for them, and re-layouts: 1.74 us -> 4.54 us
    slice x3 -> x1, local copies, waits for them, and re-layouts: 6.68 us -> 3.97 us  [on_device(): noise_draws[0, 1]]
    reshape x4 -> x0, local copies, waits for them, and re-layouts: 2.7 us -> none  [the longest x1 0.74 us: on_device(): halo_send.reshape(-1, 1)]
where the time goes in v2:
time: 187 us; the launch traced here: 184 us
  Pallas kernels  171 us (91%)
  local copies, waits for them, and re-layouts  9.96 us (5%)
  between operations  2.19 us (1%)
    pallas_call x1, Pallas kernels, run_net(): pl.pallas_call(functools.partial(net_kernel, tuple(scratch), gathered), o...  168 us
    unnamed x9, local copies, waits for them, and re-layouts  4.54 us
    slice x1, local copies, waits for them, and re-layouts, on_device(): noise_draws[0, 1]  3.97 us

profile of v2, /device:TPU:0, one launch (start us, length us, event | category | flops | bytes accessed | tf_op | source)
XLA Modules:
  0.0 184.1 jit_solution(10997025153891836867)
XLA Ops:
  1.9 1.4 fusion.3
  3.4 1.4 copy.74
  4.8 4.0 %fusion.2 = (f32[1,1,84,3072]{3,1,2,0:T(1,128)S(1)}, f32[1,1,84,3072]{3,1,2,0:T(1,128)S(1)}) fusion(f32[1,2,84,3072]{3,1,2,0:T(2,128)} %param.33), kind=kLoop, calls=%fused_computation.7 | loop fusion | bytes 4128768 | tf_op jit(solution)/shard_map/slice | solution.py:855
  8.8 0.0 copy-start
  8.8 0.0 copy-start.2
  8.8 1.2 copy.73
  10.0 0.2 copy-done
  10.2 0.0 copy-done.2
  10.2 0.0 copy-start.1
  10.2 1.3 fusion.1.noisy
  11.6 0.0 copy-done.1
  11.6 1.7 copy_bitcast_fusion.1
  13.3 167.7 %shard_map.478 = (f32[16,2560]{1,0:T(8,128)}, f32[16,2048]{1,0:T(8,128)}, f32[64,512]{1,0:T(8,128)}, f32[8,128]{1,0:T(8,128)}) custom-call(f32[1,2]{1,0:T(1,128)} %levels.1, s32[1]{0:T(128)} %bitcast.32.node_count, s32[1]{0:T(128)} %bitcast.33.pixel_count, f32[84,3072]{1,0:T(8,128)} %get-tuple-element.85.previous, f32[84,3072]{1,0:T(8,128)} %fusion.1.noisy, ...), custom_call_target="tpu_custom_call" | custom-call | tf_op jit(solution)/shard_map/pallas_call | solution.py:762
  181.0 2.9 %shard_map.479 = (f32[16,168]{1,0:T(8,128)}, f32[16,168]{1,0:T(8,128)}, f32[16,168]{1,0:T(8,128)}, f32[16,1536]{1,0:T(8,128)}, f32[16,1536]{1,0:T(8,128)}, /*ind...) custom-call(f32[8,128]{1,0:T(8,128)} %get-tuple-element.52.totals, ...), custom_call_target="tpu_custom_call" | custom-call | tf_op jit(solution)/shard_map/pallas_call | solution.py:813
Async XLA Ops:
  8.8 1.4 copy-start
  8.8 1.4 copy-start.2
  10.2 1.4 copy-start.1

commit v3 on v2

--- a/solution.py
+++ b/solution.py
@@ -132,7 +132,7 @@
         w_down=pltpu.VMEM(GRID + (hidden // 32, width), LOW),
         loads=pltpu.SemaphoreType.DMA((7,)),
         ready=pltpu.SemaphoreType.REGULAR((2,)),
-        fold=pltpu.SemaphoreType.DMA((2, 6, 4, 3)),
+        fold=pltpu.SemaphoreType.DMA((2, 6, 4, 4)),
         small=pltpu.SemaphoreType.DMA((2, 12)),
         links=pltpu.SemaphoreType.DMA((2, 4, 2)),
         spread=pltpu.SemaphoreType.DMA((2, 6, 4, 3)),
@@ -211,58 +211,56 @@
 
 
 class Fold:
-    def __init__(self, sources, rooms, outs, sems, first, where):
+    def __init__(self, sources, rooms, outs, spans, sems, first, where):
         self.sources, self.rooms, self.outs, self.sems, self.first = sources, rooms, outs, sems, first
         self.z, self.y, self.x, self.c, self.sibling, self.across_x, self.across_y, _ = where
         self.far = far_planes(self.z)
+        self.spans = [(i, slice(a, b), slice(a, (a + b) // 2), slice((a + b) // 2, b)) for i, (a, b) in enumerate(spans)]
         self.near, self.one, self.two, self.last = {}, {}, {}, []
 
     def start(self, k):
         p = self.far[k]
-        for i, (g, room) in enumerate(zip(self.sources, self.rooms)):
+        for g, room, (i, cols, lower, upper) in zip(self.sources, self.rooms, self.spans):
             self.near[k, i] = send(
-                g.at[p, :, :, 1 - self.c], room.at[p, :, :, 0], self.sems, (0, k, self.first + i), self.sibling)
+                g.at[p, :, :, 1 - self.c, :, cols], room.at[p, :, :, 0, :, cols], self.sems, (0, k, self.first + i), self.sibling)
 
     def chip(self, k):
         p = self.far[k]
-        for i, (g, room) in enumerate(zip(self.sources, self.rooms)):
-            h = g.shape[-1] // 2
+        for g, room, (i, cols, lower, upper) in zip(self.sources, self.rooms, self.spans):
             self.near[k, i].wait_recv()
-            room[p, :, :, 0] = plus(g[p, :, :, self.c], room[p, :, :, 0]).astype(LOW)
-            self.one[k, i, 0] = send(room.at[p, :, 1 - self.x, 0, :, :h], room.at[p, 0, :, 1, :, :h], self.sems,
+            room[p, :, :, 0, :, cols] = plus(g[p, :, :, self.c, :, cols], room[p, :, :, 0, :, cols]).astype(LOW)
+            self.one[k, i, 0] = send(room.at[p, :, 1 - self.x, 0, :, lower], room.at[p, 0, :, 1, :, lower], self.sems,
                                      (1, k, self.first + i), self.across_x)
-            self.one[k, i, 1] = send(room.at[p, 1 - self.y, :, 0, :, h:], room.at[p, 0, :, 1, :, h:], self.sems,
+            self.one[k, i, 1] = send(room.at[p, 1 - self.y, :, 0, :, upper], room.at[p, 0, :, 1, :, upper], self.sems,
                                      (2, k, self.first + i), self.across_y)
 
     def turn(self, k):
         p = self.far[k]
-        for i, room in enumerate(self.rooms):
-            h = room.shape[-1] // 2
+        for room, (i, cols, lower, upper) in zip(self.rooms, self.spans):
             self.one[k, i, 0].wait_recv()
-            room[p, 0, :, 1, :, :h] = plus(room[p, :, self.x, 0, :, :h], room[p, 0, :, 1, :, :h]).astype(LOW)
-            self.two[k, i, 0] = send(room.at[p, 0, 1 - self.y, 1, :, :h], room.at[p, 1, 0, 1, :, :h], self.sems,
+            room[p, 0, :, 1, :, lower] = plus(room[p, :, self.x, 0, :, lower], room[p, 0, :, 1, :, lower]).astype(LOW)
+            self.two[k, i, 0] = send(room.at[p, 0, 1 - self.y, 1, :, lower], room.at[p, 1, 0, 1, :, lower], self.sems,
                                      (3, k, self.first + i), self.across_y)
             self.one[k, i, 1].wait_recv()
-            room[p, 0, :, 1, :, h:] = plus(room[p, self.y, :, 0, :, h:], room[p, 0, :, 1, :, h:]).astype(LOW)
-            self.two[k, i, 1] = send(room.at[p, 0, 1 - self.x, 1, :, h:], room.at[p, 1, 0, 1, :, h:], self.sems,
+            room[p, 0, :, 1, :, upper] = plus(room[p, self.y, :, 0, :, upper], room[p, 0, :, 1, :, upper]).astype(LOW)
+            self.two[k, i, 1] = send(room.at[p, 0, 1 - self.x, 1, :, upper], room.at[p, 1, 0, 1, :, upper], self.sems,
                                      (4, k, self.first + i), self.across_x)
 
     def leave(self, k):
         p = self.far[k]
-        for i, (room, out) in enumerate(zip(self.rooms, self.outs)):
-            h = room.shape[-1] // 2
+        for room, out, (i, cols, lower, upper) in zip(self.rooms, self.outs, self.spans):
             self.two[k, i, 0].wait_recv()
             self.two[k, i, 1].wait_recv()
-            left = plus(room[p, 0, self.y, 1, :, :h], room[p, 1, 0, 1, :, :h])
-            right = plus(room[p, 0, self.x, 1, :, h:], room[p, 1, 0, 1, :, h:])
+            left = plus(room[p, 0, self.y, 1, :, lower], room[p, 1, 0, 1, :, lower])
+            right = plus(room[p, 0, self.x, 1, :, upper], room[p, 1, 0, 1, :, upper])
             if k == 3:
-                out[:, :h] = left
-                out[:, h:] = right
+                out[:, lower] = left
+                out[:, upper] = right
                 continue
-            room[p, 1, 0, 1, :, :h] = left.astype(LOW)
-            room[p, 1, 0, 1, :, h:] = right.astype(LOW)
+            room[p, 1, 0, 1, :, lower] = left.astype(LOW)
+            room[p, 1, 0, 1, :, upper] = right.astype(LOW)
             copy = pltpu.make_async_remote_copy(
-                src_ref=room.at[p, 1, 0, 1], dst_ref=room.at[self.z, 1, 1, 1],
+                src_ref=room.at[p, 1, 0, 1, :, cols], dst_ref=room.at[self.z, 1, 1, 1, :, cols],
                 send_sem=self.sems.at[0, 5, k, self.first + i], recv_sem=self.sems.at[1, 5, self.z, self.first + i],
                 device_id={"patch": p * 2 + self.y, "rep": self.x * 2 + self.c}, device_id_type=MESH,
             )
@@ -270,15 +268,15 @@
             self.last.append(copy)
 
     def end(self):
-        for i, (room, out) in enumerate(zip(self.rooms, self.outs)):
+        for room, out, (i, cols, lower, upper) in zip(self.rooms, self.outs, self.spans):
             for k in range(3):
                 p = self.far[k]
-                come = room.at[p, 1, 1, 1]
+                come = room.at[p, 1, 1, 1, :, cols]
                 pltpu.make_async_remote_copy(
                     src_ref=come, dst_ref=come, send_sem=self.sems.at[0, 5, k, self.first + i],
                     recv_sem=self.sems.at[1, 5, p, self.first + i], device_id=self.sibling, device_id_type=MESH,
                 ).wait_recv()
-                out[...] = plus(out[...], room[p, 1, 1, 1])
+                out[:, cols] = plus(out[:, cols], room[p, 1, 1, 1, :, cols])
 
     def drain(self):
         for copy in list(self.near.values()) + list(self.one.values()) + list(self.two.values()) + self.last:
@@ -296,7 +294,7 @@
     near = nodes + 2 * halo
     width, hidden = r.start.shape[1], r.gated.shape[1]
     at = [0, 3 * width, 4 * width, 4 * width + hidden, 4 * width + hidden + 256, 4 * width + hidden + 384]
-    tile = 1024
+    tile = 1536
     tiles = pixels // tile
     patches = lax.axis_size("patch")
     me = lax.axis_index("patch")
@@ -451,14 +449,14 @@
         r.start[...] = nt(r.sums[rows], early(3, 5)) * r.inv_count[...]
 
         def norm(b):
-            part = block(b, 64)
+            part = block(b, 256)
             unit, inverse = norm_parts(r.start[part])
             r.unit_one[s, part] = unit.astype(LOW)
             r.inv_one[s, part] = inverse
             scaled = unit * (1.0 + r.wave[s, 0:1]) + r.wave[s, 1:2]
-            r.normed[pl.ds(pl.multiple_of(s * nodes + b * 64, 64), 64)] = scaled.astype(LOW)
-
-        loop(nodes // 64, norm)
+            r.normed[pl.ds(pl.multiple_of(s * nodes + b * 256, 256), 256)] = scaled.astype(LOW)
+
+        loop(nodes // 256, norm)
         normed = r.normed[rows]
         r.outgoing[s] = tn(r.send_hot[...], normed).astype(LOW)
         first = 2 * nodes + 2 * halo * s
@@ -507,14 +505,14 @@
         r.start[...] += nn(r.mixed[rows], early(2, 3))
 
         def norm(b):
-            part = block(b, 64)
+            part = block(b, 256)
             unit, inverse = norm_parts(r.start[part])
             r.unit_two[s, part] = unit.astype(LOW)
             r.inv_two[s, part] = inverse
             scaled = unit * (1.0 + r.wave[s, 2:3]) + r.wave[s, 3:4]
-            r.second[pl.ds(pl.multiple_of(s * nodes + b * 64, 64), 64)] = scaled.astype(LOW)
-
-        loop(nodes // 64, norm)
+            r.second[pl.ds(pl.multiple_of(s * nodes + b * 256, 256), 256)] = scaled.astype(LOW)
+
+        loop(nodes // 256, norm)
 
         def feed(j):
             cols = block(j, 256)
@@ -588,7 +586,7 @@
         r.d_wave[s, which : which + 2] = jnp.zeros((2, width), WIDE)
 
         def norm(b):
-            part = block(b, 64)
+            part = block(b, 256)
             unit = units[s, part].astype(WIDE)
             d_out = r.scores[part, :width]
             d_scale = jnp.sum(d_out * unit, axis=0, keepdims=True)
@@ -600,7 +598,7 @@
             d_hidden = d_unit - jnp.mean(d_unit, axis=-1, keepdims=True) - unit * along
             r.start[part] += inverses[s, part] * d_hidden
 
-        loop(nodes // 64, norm)
+        loop(nodes // 256, norm)
 
     def absorb(s, copies):
         rows = slice(s * nodes, (s + 1) * nodes)
@@ -611,8 +609,10 @@
         r.d_summed[rows] = (r.start[...] * r.inv_count[...]).astype(LOW)
 
     if not gathered:
-        late = Fold((r.g_up, r.g_down), (r.w_up, r.w_down), outs[1:3], r.fold, 1, where)
-        soon_fold = Fold((r.g_early,), (r.w_early,), outs[:1], r.fold, 0, where)
+        late = Fold((r.g_up, r.g_down), (r.w_up, r.w_down), outs[1:3], ((0, hidden), (0, width)), r.fold, 1, where)
+        cut = 4 * width
+        soon_fold = Fold((r.g_early,), (r.w_early,), outs[:1], ((0, cut),), r.fold, 0, where)
+        tail_fold = Fold((r.g_early,), (r.w_early,), outs[:1], ((cut, cut + width),), r.fold, 3, where)
     fold_steps = []
 
     def announce(which):
@@ -696,8 +696,16 @@
         put_early(i, w_at[2], tn(r.mixed[:, cols], r.d_attn[...]))
         put_early(i, w_at[5], tn(r.final[:, cols], r.taken[...]))
         advance(fold_steps, 1)
+    advance(fold_steps, len(fold_steps))
+    if not gathered:
+        pl.semaphore_wait(r.ready.at[1], len(folders))
+        for k in range(4):
+            soon_fold.start(k)
+        for k in range(4):
+            soon_fold.chip(k)
     absorb(0, copies)
-    advance(fold_steps, len(fold_steps))
+    if not gathered:
+        soon_fold.turn(0)
     for i in range(2):
         put_early(i, w_at[3], tn(r.d_summed[:, i * width // 2 : (i + 1) * width // 2], r.sums[...]))
         total = jnp.zeros((16, 16, 128), WIDE)
@@ -716,18 +724,25 @@
         outs[3][...] = r.lost[...]
         return
 
-    pl.semaphore_wait(r.ready.at[1], len(folders))
     for k in range(4):
-        soon_fold.start(k)
+        tail_fold.start(k)
+    soon_fold.turn(1)
     for k in range(4):
-        soon_fold.chip(k)
+        tail_fold.chip(k)
+    soon_fold.leave(0)
+    soon_fold.turn(2)
+    soon_fold.leave(1)
+    soon_fold.turn(3)
+    for k in range(4):
+        tail_fold.turn(k)
+    soon_fold.leave(2)
     late.end()
     squares = jnp.sum(outs[1][...] * outs[1][...]) + jnp.sum(outs[2][...] * outs[2][...])
+    soon_fold.leave(3)
     for k in range(4):
-        soon_fold.turn(k)
-    for k in range(4):
-        soon_fold.leave(k)
+        tail_fold.leave(k)
     soon_fold.end()
+    tail_fold.end()
     squares = squares + jnp.sum(outs[0][...] * outs[0][...])
     row = lax.broadcasted_iota(jnp.int32, (8, 128), 0)
     live = (chan * jnp.minimum(pixel_count[0], pixels)).astype(WIDE)
@@ -745,6 +760,7 @@
     outs[3][...] = r.board[8] + r.board[9] + r.board[10] + r.board[11]
     late.drain()
     soon_fold.drain()
+    tail_fold.drain()
     for copy in more + level_copies:
         copy.wait_send()
 

time: 187 us -> 177 us (0.947)
  Pallas kernels: 171 us -> 160 us
    pallas_call x1, Pallas kernels: 168 us -> 158 us  [run_net(): pl.pallas_call(functools.partial(net_kernel, tuple(scratch), gathered), o...]
where the time goes in v3:
time: 177 us; the launch traced here: 174 us
  Pallas kernels  160 us (90%)
  local copies, waits for them, and re-layouts  9.96 us (6%)
  between operations  2.19 us (1%)
    pallas_call x1, Pallas kernels, run_net(): pl.pallas_call(functools.partial(net_kernel, tuple(scratch), gathered), o...  158 us
    unnamed x9, local copies, waits for them, and re-layouts  4.54 us
    slice x1, local copies, waits for them, and re-layouts, on_device(): noise_draws[0, 1]  3.97 us

profile of v3, /device:TPU:0, one launch (start us, length us, event | category | flops | bytes accessed | tf_op | source)
XLA Modules:
  0.0 174.0 jit_solution(14455370482145155272)
XLA Ops:
  1.9 1.4 fusion.3
  3.4 1.4 copy.74
  4.8 4.0 %fusion.2 = (f32[1,1,84,3072]{3,1,2,0:T(1,128)S(1)}, f32[1,1,84,3072]{3,1,2,0:T(1,128)S(1)}) fusion(f32[1,2,84,3072]{3,1,2,0:T(2,128)} %param.33), kind=kLoop, calls=%fused_computation.7 | loop fusion | bytes 4128768 | tf_op jit(solution)/shard_map/slice | solution.py:871
  8.8 0.0 copy-start
  8.8 0.0 copy-start.2
  8.8 1.2 copy.73
  10.0 0.2 copy-done
  10.2 0.0 copy-done.2
  10.2 0.0 copy-start.1
  10.2 1.3 fusion.1.noisy
  11.6 0.0 copy-done.1
  11.6 1.7 copy_bitcast_fusion.1
  13.3 157.6 %shard_map.478 = (f32[16,2560]{1,0:T(8,128)}, f32[16,2048]{1,0:T(8,128)}, f32[64,512]{1,0:T(8,128)}, f32[8,128]{1,0:T(8,128)}) custom-call(f32[1,2]{1,0:T(1,128)} %levels.1, s32[1]{0:T(128)} %bitcast.32.node_count, s32[1]{0:T(128)} %bitcast.33.pixel_count, f32[84,3072]{1,0:T(8,128)} %get-tuple-element.85.previous, f32[84,3072]{1,0:T(8,128)} %fusion.1.noisy, ...), custom_call_target="tpu_custom_call" | custom-call | tf_op jit(solution)/shard_map/pallas_call | solution.py:778
  170.9 2.9 %shard_map.479 = (f32[16,168]{1,0:T(8,128)}, f32[16,168]{1,0:T(8,128)}, f32[16,168]{1,0:T(8,128)}, f32[16,1536]{1,0:T(8,128)}, f32[16,1536]{1,0:T(8,128)}, /*ind...) custom-call(f32[8,128]{1,0:T(8,128)} %get-tuple-element.52.totals, ...), custom_call_target="tpu_custom_call" | custom-call | tf_op jit(solution)/shard_map/pallas_call | solution.py:829
Async XLA Ops:
  8.8 1.4 copy-start
  8.8 1.4 copy-start.2
  10.2 1.4 copy-start.1
